TPU v7x, 32 devices: a whole 2x2x4 slice. The times are simulated.
32 devices in a mesh: col: 16 (over z, x, core), row: 2 (over y).
Axes of the slice: x: 2, y: 2, z: 4, core: 2. Of those that a mesh axis runs over, the one named last changes fastest.
Arguments:
- start_field: float32 [2, 128, 4096], P(None, 'row', 'col'), may hold values from -36 to 36
- seam_target: float32 [2, 2, 4, 32768], P(None, None, 'row', 'col'), may hold values from -6 to 6
- seam_rows: int32 [4, 4, 32768], P(None, 'row', 'col'), may hold values from 0 to 30
- seam_band: int32 [4, 4, 32768], P(None, 'row', 'col'), may hold values from 0 to 2
- seam_frac: int32 [4, 2, 4, 32768], P(None, None, 'row', 'col'), may hold values from 0 to 255
- adjacency: int32 [2, 4, 128], P(None, 'row', 'col'), may hold values 0 or 1
Outputs:
- refined_field: float32 [2, 128, 4096], P(None, 'row', 'col')
- last_residual: float32 [2, 128, 4096], P(None, 'row', 'col')
Inputs may be any that keep to these rules, and one draw needn't show every extreme that they name: `seam_rows`: index of the cell along the seam, in control points of the tile. `seam_band`: depth of the cell from the tile's edge. `seam_frac`: offsets in 256ths of a cell.
All inputs are finite; a program needn't handle non-finite values. No bound on the sum of `adjacency` on one device may be relied on, other than what follows from the above.
Results may differ from a plain program's by a relative error of at most 0.0003.
Values sent between devices are 32-bit elements; how exact they have to be, the bound alone decides.
No kernel may reach another device: no remote copies, remote signals or barrier semaphores. Data moves between devices by JAX's collectives and lax.ppermute only.
A program may use at most 64 MiB of HBM per device.

v0:
```python
import jax
import jax.numpy as jnp
from jax import lax
from jax.experimental import pallas as pl
from jax.experimental.pallas import tpu as pltpu
from jax.sharding import PartitionSpec as P

GRID = 32
BAND = 4
ITERS = 3
BEND_WEIGHT = 0.05
DAMPING = 0.5

SAMPLES = 256
LANES = 128
PACK = LANES // GRID
TILE_ROWS = 2
HALF_COLS = 4
PIECES = 3
WINDOW_COLS = PIECES * HALF_COLS
WIDTH = WINDOW_COLS * GRID
BLOCK_ROWS = TILE_ROWS * GRID
TABLE_ROWS = 32
HALF_ROWS = BLOCK_ROWS + HALF_COLS * TABLE_ROWS
BOUNDS = WINDOW_COLS - 1

LOW, HIGH = 0.5, 6.0
CENTRE, RADIUS = (HIGH + LOW) / 2, (HIGH - LOW) / 2

BASIS = ITERS + 1
PAIRS = [(i, j) for i in range(BASIS) for j in range(i, BASIS)]
SUM_ROWS = 16

F32, BF16 = jnp.float32, jnp.bfloat16


def hat(offset):
    return jnp.maximum(1.0 - jnp.abs(offset), 0.0)


def pack_kernel(adjacency, field, target, rows, band, frac, own, ahead, back):
    part = lax.axis_index("row") % 2
    not_last_col = (lax.axis_index("col") < lax.axis_size("col") - 1).astype(jnp.int32)
    not_last_row = (lax.axis_index("row") < lax.axis_size("row") - 1).astype(jnp.int32)
    tiles = 2 * HALF_COLS
    sub = lax.broadcasted_iota(jnp.int32, (8, SAMPLES), 0)
    for half in range(2):
        for comp in range(2):
            own[half, :BLOCK_ROWS, comp * LANES : (comp + 1) * LANES] = field[
                comp, :, half * LANES : (half + 1) * LANES
            ]
    for facing in range(4):
        along = rows[facing].astype(F32) + (frac[facing, 0].astype(F32) + 0.5) / 256.0
        across = band[facing].astype(F32) + (frac[facing, 1].astype(F32) + 0.5) / 256.0
        for tile in range(tiles):
            half, base = tile // HALF_COLS, BLOCK_ROWS + tile % HALF_COLS * TABLE_ROWS + 2 * facing
            lanes = slice(tile * SAMPLES, (tile + 1) * SAMPLES)
            own[half, base : base + 2, :] = along[:, lanes]
            own[half, base + 8 : base + 10, :] = across[:, lanes]
            own[half, base + 16 : base + 18, :] = target[facing // 2, facing % 2][:, lanes]
    for tile in range(tiles):
        half, base = tile // HALF_COLS, BLOCK_ROWS + tile % HALF_COLS * TABLE_ROWS + 24
        masks = jnp.zeros((8, SAMPLES), F32)
        for side in range(2):
            for row in range(TILE_ROWS):
                value = adjacency[side, row, tile]
                if side == 0 and tile == tiles - 1:
                    value = value * not_last_col
                if side == 1 and row == TILE_ROWS - 1:
                    value = value * not_last_row
                masks = jnp.where(sub == 2 * side + row, value.astype(F32), masks)
        own[half, base : base + 8, :] = masks
    ahead[...] = own[1 - part]
    back[...] = own[part]


def split(value):
    high = value.astype(BF16)
    return high, (value - high.astype(F32)).astype(BF16)


def window_kernel(pairs, *refs):
    count = 4 * pairs
    pieces = refs[:count]
    mine, theirs, sums, slots, vecs, weight_hi, weight_lo, cross, shift, flipped, spread, sems = refs[count:]
    tile_rows = 4 * pairs
    own_pair = pairs // 2
    part = lax.axis_index("row") % 2

    copies = []
    for pair in range(pairs):
        places = (
            slots.at[2 * pair + part, pl.ds(1 - part, 2)],
            slots.at[2 * pair + 1 - part, pl.ds(1 - part, 2)],
            slots.at[2 * pair + part, 2 * part],
            slots.at[2 * pair + 1 - part, 2 * part],
        )
        for kind in range(4):
            at = 4 * pair + kind
            copies.append(pltpu.make_async_copy(pieces[at], places[kind], sems.at[at]))
    for copy in copies:
        copy.start()
    for copy in copies:
        copy.wait()

    sub8 = lax.broadcasted_iota(jnp.int32, (8, LANES), 0)
    lane8 = lax.broadcasted_iota(jnp.int32, (8, LANES), 1)
    near_side = sub8 >= 4
    sub16 = lax.broadcasted_iota(jnp.int32, (16, 2 * LANES), 0)
    lane16 = lax.broadcasted_iota(jnp.int32, (16, 2 * LANES), 1)
    side16 = (lane16 < LANES) == (sub16 % 8 >= 4)
    keep = [
        jnp.where(side16 & (lane16 % LANES // GRID == unit), 1.0, 0.0).astype(BF16)
        for unit in range(PACK)
    ]

    for block in range(2 * pairs):
        for piece in range(PIECES):
            for comp in range(2):
                vecs[0, comp, block * BLOCK_ROWS : (block + 1) * BLOCK_ROWS, piece * LANES : (piece + 1) * LANES] = slots[
                    block, piece, :BLOCK_ROWS, comp * LANES : (comp + 1) * LANES
                ]

    def table(row, col, entry):
        start = BLOCK_ROWS + col % HALF_COLS * TABLE_ROWS + entry
        return slots[row // TILE_ROWS, col // HALF_COLS, start : start + 1, :]

    along_iota = lax.broadcasted_iota(jnp.int32, (GRID, SAMPLES), 0).astype(F32)
    sub_s = lax.broadcasted_iota(jnp.int32, (8, SAMPLES), 0)
    near_s = sub_s >= 4
    depth = jnp.where(near_s, 7 - sub_s, sub_s).astype(F32)

    def east_group(bound, group):
        return bound * pairs + group

    def south_group(row, group):
        return BOUNDS * pairs + row * PIECES + group

    def set_tables(index, direction, near_tiles, far_tiles):
        for unit in range(PACK):
            both = (near_tiles[unit], far_tiles[unit])
            ys = []
            for side in range(2):
                row, col = both[side]
                entry = 2 * (2 * direction + side) + row % TILE_ROWS
                weight = hat(table(row, col, entry) - along_iota)
                high, low = split(weight)
                start = side * LANES + unit * GRID
                weight_hi[index, start : start + GRID, :] = high
                weight_lo[index, start : start + GRID, :] = low
                ys.append(table(row, col, 8 + entry))
            row, col = both[0]
            mask = table(row, col, 24 + 2 * direction + row % TILE_ROWS)
            signed = jnp.where(near_s, mask, -mask)
            cross[index, 8 * unit : 8 * unit + 8, :] = hat(jnp.where(near_s, ys[0], ys[1]) - depth) * signed
            for comp in range(2):
                shift[index, 2 * unit + comp : 2 * unit + comp + 1, :] = table(
                    row, col, 16 + 4 * direction + 2 * comp + row % TILE_ROWS
                )

    for bound in range(BOUNDS):
        for group in range(pairs):
            tiles = [(4 * group + unit, bound) for unit in range(PACK)]
            set_tables(east_group(bound, group), 0, tiles, [(row, col + 1) for row, col in tiles])
    for row in range(tile_rows - 1):
        for group in range(PIECES):
            tiles = [(row, 4 * group + unit) for unit in range(PACK)]
            set_tables(south_group(row, group), 1, tiles, [(at + 1, col) for at, col in tiles])

    spread[...] = jnp.zeros_like(spread)

    def seam_group(index, strips, first):
        high, low = split(jnp.concatenate(strips, axis=0))
        high = jnp.concatenate([high, high], axis=1)
        low = jnp.concatenate([low, low], axis=1)
        left_hi = jnp.concatenate([high * keep[unit] for unit in range(PACK)], axis=0)
        left_lo = jnp.concatenate([low * keep[unit] for unit in range(PACK)], axis=0)
        w_hi, w_lo = weight_hi[index], weight_lo[index]
        gathered = (
            jnp.dot(left_hi, w_hi, preferred_element_type=F32)
            + jnp.dot(left_lo, w_hi, preferred_element_type=F32)
            + jnp.dot(left_hi, w_lo, preferred_element_type=F32)
        )
        pulled = []
        for unit in range(PACK):
            across = cross[index, 8 * unit : 8 * unit + 8, :]
            for comp in range(2):
                at = 2 * unit + comp
                total = jnp.sum(gathered[8 * at : 8 * at + 8] * across, axis=0, keepdims=True)
                if first:
                    total = total - shift[index, at : at + 1, :]
                pulled.append(total * across)
        right_hi, right_lo = split(jnp.concatenate(pulled, axis=0))
        numbers = (((1,), (1,)), ((), ()))
        back = (
            lax.dot_general(right_hi, w_hi, numbers, preferred_element_type=F32)
            + lax.dot_general(right_lo, w_hi, numbers, preferred_element_type=F32)
            + lax.dot_general(right_hi, w_lo, numbers, preferred_element_type=F32)
        )
        result = []
        for comp in range(2):
            out = None
            for unit in range(PACK):
                at = 8 * (2 * unit + comp)
                chosen = jnp.where(near_side, back[at : at + 8, :LANES], back[at : at + 8, LANES:])
                out = chosen if out is None else jnp.where(lane8 // GRID == unit, chosen, out)
            result.append(out)
        return result

    sub32 = lax.broadcasted_iota(jnp.int32, (GRID, LANES), 0)
    lane32 = lax.broadcasted_iota(jnp.int32, (GRID, LANES), 1) % GRID
    inner = (sub32 >= 1) & (sub32 <= GRID - 2) & (lane32 >= 1) & (lane32 <= GRID - 2)

    def laplacian(value):
        return (
            pltpu.roll(value, 1, 0)
            + pltpu.roll(value, GRID - 1, 0)
            + pltpu.roll(value, 1, 1)
            + pltpu.roll(value, LANES - 1, 1)
            - 4.0 * value
        )

    def apply(step, scale, own_weight, last_weight):
        for comp in range(2):
            for group in range(pairs):
                for piece in range(PIECES):
                    flipped[comp, piece * LANES : (piece + 1) * LANES, group * LANES : (group + 1) * LANES] = vecs[
                        step, comp, group * LANES : (group + 1) * LANES, piece * LANES : (piece + 1) * LANES
                    ].T
        for bound in range(step, BOUNDS - step):
            at = GRID * bound + GRID - 8
            for group in range(pairs):
                lanes = slice(group * LANES, (group + 1) * LANES)
                strips = [
                    jnp.where(near_side, flipped[comp, at : at + 8, lanes], flipped[comp, at + 8 : at + 16, lanes])
                    for comp in range(2)
                ]
                result = seam_group(east_group(bound, group), strips, step == 0)
                for comp in range(2):
                    spread[comp, at : at + 8, lanes] = jnp.where(near_side, result[comp], 0.0)
                    spread[comp, at + 8 : at + 16, lanes] = jnp.where(near_side, 0.0, result[comp])
        used = (1,) if step == ITERS else range(PIECES)
        for piece in used:
            lanes = slice(piece * LANES, (piece + 1) * LANES)
            for comp in range(2):
                for group in range(pairs):
                    turned = spread[comp, lanes, group * LANES : (group + 1) * LANES].T
                    for unit in range(PACK):
                        start = group * LANES + unit * GRID
                        value = vecs[step, comp, start : start + GRID, lanes]
                        curved = laplacian(jnp.where(inner, laplacian(value), 0.0))
                        out = scale * (turned[unit * GRID : (unit + 1) * GRID] + BEND_WEIGHT * curved)
                        if own_weight:
                            out = out + own_weight * value
                        if last_weight:
                            out = out + last_weight * vecs[step - 1, comp, start : start + GRID, lanes]
                        vecs[step + 1, comp, start : start + GRID, lanes] = out
            for row in range(tile_rows - 1):
                at = GRID * row + GRID - 8
                strips = [
                    jnp.where(near_side, vecs[step, comp, at : at + 8, lanes], vecs[step, comp, at + 8 : at + 16, lanes])
                    for comp in range(2)
                ]
                result = seam_group(south_group(row, piece), strips, step == 0)
                for comp in range(2):
                    vecs[step + 1, comp, at : at + 8, lanes] += jnp.where(near_side, scale * result[comp], 0.0)
                    vecs[step + 1, comp, at + 8 : at + 16, lanes] += jnp.where(near_side, 0.0, scale * result[comp])

    apply(0, -1.0, 0.0, 0.0)
    apply(1, 1.0 / RADIUS, (DAMPING - CENTRE) / RADIUS, 0.0)
    apply(2, 2.0 / RADIUS, 2.0 * (DAMPING - CENTRE) / RADIUS, -1.0)
    apply(3, 2.0 / RADIUS, 2.0 * (DAMPING - CENTRE) / RADIUS, -1.0)

    first_row = own_pair * 2 * BLOCK_ROWS
    partial = [jnp.zeros((8, LANES), F32) for _ in PAIRS]
    for comp in range(2):
        for row in range(first_row, first_row + 2 * BLOCK_ROWS, 8):
            values = [vecs[1 + k, comp, row : row + 8, LANES : 2 * LANES] for k in range(BASIS)]
            for n, (i, j) in enumerate(PAIRS):
                partial[n] = partial[n] + values[i] * values[j]
    rows = [jnp.sum(value, axis=0, keepdims=True) for value in partial]
    rows.append(jnp.zeros((SUM_ROWS - len(rows), LANES), F32))
    sums[...] = jnp.concatenate(rows, axis=0)
    for k in range(BASIS):
        for comp in range(2):
            for out, block in ((mine, part), (theirs, 1 - part)):
                start = pl.multiple_of(first_row + block * BLOCK_ROWS, BLOCK_ROWS)
                out[k, comp] = vecs[1 + k, comp, pl.ds(start, BLOCK_ROWS), LANES : 2 * LANES]


def final_kernel(sums, mine, other, field, control, residual):
    part = lax.axis_index("row") % 2
    totals = jnp.sum(sums[...], axis=1, keepdims=True)
    gram = {}
    for n, (i, j) in enumerate(PAIRS):
        gram[i, j] = gram[j, i] = jnp.broadcast_to(totals[n : n + 1], (1, LANES))

    def inner(left, right):
        return sum(
            left[i] * sum(gram[i, j] * right[j] for j in right) for i in left
        )

    def image(vec):
        out = {}

        def add(at, value):
            out[at] = out[at] + value if at in out else value

        for k, value in vec.items():
            add(k, CENTRE * value)
            if k == 0:
                add(1, RADIUS * value)
            else:
                add(k - 1, RADIUS / 2 * value)
                add(k + 1, RADIUS / 2 * value)
        return out

    one = jnp.ones((1, LANES), F32)
    resid, direction, update = {0: one}, {0: one}, {}
    norm = gram[0, 0]
    for iteration in range(ITERS):
        moved = image(direction)
        step = norm / inner(direction, moved)
        for k, value in direction.items():
            update[k] = update[k] + step * value if k in update else step * value
        resid = {k: (resid[k] if k in resid else 0.0) - step * value for k, value in moved.items()}
        if iteration < ITERS - 1:
            after = inner(resid, resid)
            ratio = after / norm
            direction = {k: value + ratio * direction[k] if k in direction else value for k, value in resid.items()}
            norm = after

    for source, half in ((mine, part), (other, 1 - part)):
        lanes = pl.ds(pl.multiple_of(half * LANES, LANES), LANES)
        for comp in range(2):
            basis = [source[k, comp] for k in range(BASIS)]
            control[comp, :, lanes] = field[comp, :, lanes] + sum(update[k] * basis[k] for k in update)
            residual[comp, :, lanes] = sum(resid[k] * basis[k] for k in resid)


def shards(start_field, seam_target, seam_rows, seam_band, seam_frac, adjacency):
    row_count, col_count = lax.axis_size("row"), lax.axis_size("col")
    axes = ("col", "row")
    vmem = pl.BlockSpec(memory_space=pltpu.VMEM)
    anywhere = pl.BlockSpec(memory_space=pl.ANY)
    limit = pltpu.CompilerParams(vmem_limit_bytes=48 * 1024 * 1024)

    def shifted(value, move):
        sources = [(col, row) for col in range(col_count) for row in range(row_count)]
        perm = []
        for col, row in sources:
            to_col, to_row = move(col, row)
            if 0 <= to_col < col_count and 0 <= to_row < row_count:
                perm.append((col * row_count + row, to_col * row_count + to_row))
        return lax.ppermute(value, axes, perm)

    half = jax.ShapeDtypeStruct((HALF_ROWS, SAMPLES), F32)
    own, ahead, back = pl.pallas_call(
        pack_kernel,
        out_shape=(jax.ShapeDtypeStruct((2, HALF_ROWS, SAMPLES), F32), half, half),
        in_specs=[pl.BlockSpec(memory_space=pltpu.SMEM)] + [vmem] * 5,
        out_specs=(vmem, vmem, vmem),
        name="pack",
    )(adjacency, start_field, seam_target, seam_rows, seam_band, seam_frac)

    outward = lambda row: 1 - 2 * (row % 2)
    pieces = (
        own,
        shifted(own, lambda col, row: (col, row ^ 1)),
        shifted(ahead, lambda col, row: (col + outward(row), row)),
        shifted(back, lambda col, row: (col - outward(row), row ^ 1)),
    )
    if row_count > 2:
        from_above = [shifted(piece, lambda col, row: (col, row + 2)) for piece in pieces]
        from_below = [shifted(piece, lambda col, row: (col, row - 2)) for piece in pieces]
        pieces = (*from_above, *pieces, *from_below)
    pairs = len(pieces) // 4
    groups = BOUNDS * pairs + (4 * pairs - 1) * PIECES

    part_shape = jax.ShapeDtypeStruct((BASIS, 2, BLOCK_ROWS, LANES), F32)
    mine, theirs, sums = pl.pallas_call(
        lambda *refs: window_kernel(pairs, *refs),
        out_shape=(part_shape, part_shape, jax.ShapeDtypeStruct((SUM_ROWS, LANES), F32)),
        in_specs=[anywhere] * len(pieces),
        out_specs=(vmem, vmem, vmem),
        scratch_shapes=[
            pltpu.VMEM((2 * pairs, PIECES, HALF_ROWS, SAMPLES), F32),
            pltpu.VMEM((BASIS + 1, 2, 4 * pairs * GRID, WIDTH), F32),
            pltpu.VMEM((groups, 2 * LANES, SAMPLES), BF16),
            pltpu.VMEM((groups, 2 * LANES, SAMPLES), BF16),
            pltpu.VMEM((groups, 8 * PACK, SAMPLES), F32),
            pltpu.VMEM((groups, 2 * PACK, SAMPLES), F32),
            pltpu.VMEM((2, WIDTH, pairs * LANES), F32),
            pltpu.VMEM((2, WIDTH, pairs * LANES), F32),
            pltpu.SemaphoreType.DMA((len(pieces),)),
        ],
        compiler_params=limit,
        name="window",
    )(*pieces)

    other = shifted(theirs, lambda col, row: (col, row ^ 1))
    for axis, size in (("col", col_count), ("row", row_count)):
        if size & (size - 1):
            sums = lax.psum(sums, axis)
            continue
        hop = 1
        while hop < size:
            sums = sums + lax.ppermute(sums, axis, [(at, at ^ hop) for at in range(size)])
            hop *= 2

    out = jax.ShapeDtypeStruct(start_field.shape, F32)
    return pl.pallas_call(
        final_kernel,
        out_shape=(out, out),
        in_specs=[vmem] * 4,
        out_specs=(vmem, vmem),
        name="final",
    )(sums, mine, other, start_field)


def solution(mesh):
    placed = (
        P(None, "row", "col"),
        P(None, None, "row", "col"),
        P(None, "row", "col"),
        P(None, "row", "col"),
        P(None, None, "row", "col"),
        P(None, "row", "col"),
    )
    return jax.shard_map(
        shards,
        mesh=mesh,
        in_specs=placed,
        out_specs=(P(None, "row", "col"), P(None, "row", "col")),
        check_vma=False,
    )
```

profile of v0, /device:TPU:0, one launch (start us, length us, event | category | flops | bytes accessed | tf_op | source)
XLA Modules:
  0.0 56.7 jit_solution(6504449535851845043)
XLA Ops:
  0.6 2.1 %pack.1 = (f32[2,192,256]{2,1,0:T(8,128)}, f32[192,256]{1,0:T(8,128)}, f32[192,256]{1,0:T(8,128)}) custom-call(s32[2,2,8]{2,1,0:T(2,128)} %adjacency.1, f32[2,64,256]{2,1,0:T(8,128)} %field.3, f32[2,2,2,2048]{3,2,1,0:T(2,128)} %target.1, s32[4,2,2048]{2,1,0:T(2,128)} %rows.1, s32[4,2,2048]{2,1,0:T(2,128)} %band.1, s32[4,2,2,2048]{3,2,1,0:T(2,128)} %frac.1), custom_call_target="tpu_custom_call" | custom-call | tf_op jit(solution)/shard_map/pack/pallas_call | solution.py:358
  2.8 3.0 %collective-permute-start = (f32[2,192,256]{2,1,0:T(8,128)}, f32[2,192,256]{2,1,0:T(8,128)S(1)}, u32[]{:S(2)}, u32[]{:S(2)}) collective-permute-start(f32[2,192,256]{2,1,0:T(8,128)} %get-tuple-element.8.refs_0_), channel_id=1, source_target_pairs={{0,1},{1,0},{2,3},{3,2},{4,5},{5,4},{6,7},{7,6},{8,9},{9,8},{10,11... | collective-permute-start | bytes 1179656 | tf_op jit(solution)/shard_map/ppermute | solution.py:355
  5.7 1.5 %collective-permute-start.1 = (f32[192,256]{1,0:T(8,128)}, f32[192,256]{1,0:T(8,128)S(1)}, u32[]{:S(2)}, u32[]{:S(2)}) collective-permute-start(f32[192,256]{1,0:T(8,128)} %get-tuple-element.9), channel_id=1, source_target_pairs={{0,2},{2,4},{3,1},{4,6},{5,3},{6,8},{7,5},{8,10},{9,7},{10,12},{11... | collective-permute-start | bytes 589832 | tf_op jit(solution)/shard_map/ppermute | solution.py:355
  7.2 0.7 %collective-permute-start.2 = (f32[192,256]{1,0:T(8,128)}, f32[192,256]{1,0:T(8,128)S(1)}, u32[]{:S(2)}, u32[]{:S(2)}) collective-permute-start(f32[192,256]{1,0:T(8,128)} %get-tuple-element.10), channel_id=1, source_target_pairs={{1,2},{2,1},{3,4},{4,3},{5,6},{6,5},{7,8},{8,7},{9,10},{10,9},{11,... | collective-permute-start | bytes 589832 | tf_op jit(solution)/shard_map/ppermute | solution.py:355
  7.9 0.6 %collective-permute-done.1.refs_2_ = f32[192,256]{1,0:T(8,128)S(1)} collective-permute-done((f32[192,256]{1,0:T(8,128)}, f32[192,256]{1,0:T(8,128)S(1)}, u32[]{:S(2)}, u32[]{:S(2)}) %collective-permute-start.1) | collective-permute-done | bytes 196640 | tf_op jit(solution)/shard_map/ppermute | solution.py:355
  8.4 0.0 collective-permute-done.2.refs_3_
  8.4 9.2 %collective-permute-done.refs_1_ = f32[2,192,256]{2,1,0:T(8,128)S(1)} collective-permute-done((f32[2,192,256]{2,1,0:T(8,128)}, f32[2,192,256]{2,1,0:T(8,128)S(1)}, u32[]{:S(2)}, u32[]{:S(2)}) %collective-permute-start) | collective-permute-done | bytes 393248 | tf_op jit(solution)/shard_map/ppermute | solution.py:355
  17.7 1.0 %copy-done = f32[2,192,256]{2,1,0:T(8,128)S(1)} copy-done((f32[2,192,256]{2,1,0:T(8,128)S(1)}, f32[2,192,256]{2,1,0:T(8,128)}, u32[]{:S(2)}) %copy-start) | copy-done | bytes 393240
  18.7 14.0 %window.1 = (f32[4,2,64,128]{3,2,1,0:T(8,128)S(1)}, f32[4,2,64,128]{3,2,1,0:T(8,128)S(1)}, f32[16,128]{1,0:T(8,128)S(1)}) custom-call(f32[2,192,256]{2,1,0:T(8,128)S(1)} %copy-done, f32[2,192,256]{2,1,0:T(8,128)S(1)} %collective-permute-done.refs_1_, f32[192,256]{1,0:T(8,128)S(1)} %collective-permute-done.1.refs_2_, ...), custom_call_target="tpu_custom_call" | custom-call | tf_op jit(solution)/shard_map/window/pallas_call | solution.py:381
  32.7 0.7 %copy-done.1 = f32[4,2,64,128]{3,2,1,0:T(8,128)} copy-done((f32[4,2,64,128]{3,2,1,0:T(8,128)}, f32[4,2,64,128]{3,2,1,0:T(8,128)S(1)}, u32[]{:S(2)}) %copy-start.1) | copy-done | bytes 262168
  33.4 3.3 %collective-permute-start.8 = (f32[4,2,64,128]{3,2,1,0:T(8,128)S(1)}, f32[4,2,64,128]{3,2,1,0:T(8,128)S(1)}, u32[]{:S(2)}, u32[]{:S(2)}) collective-permute-start(f32[4,2,64,128]{3,2,1,0:T(8,128)S(1)} %get-tuple-element.13), channel_id=1, source_target_pairs={{0,1},{1,0},{2,3},{3,2},{4,5},{5,4},{6,7},{7,6},{8,9},{9,8},{10,11... | collective-permute-start | bytes 786440 | tf_op jit(solution)/shard_map/ppermute | solution.py:355
  36.7 0.0 collective-permute-start.3
  36.7 1.2 %collective-permute-done.3 = f32[16,128]{1,0:T(8,128)S(1)} collective-permute-done((f32[16,128]{1,0:T(8,128)S(1)}, f32[16,128]{1,0:T(8,128)S(1)}, u32[]{:S(2)}, u32[]{:S(2)}) %collective-permute-start.3) | collective-permute-done | bytes 8224 | tf_op jit(solution)/shard_map/ppermute | solution.py:408
  37.9 1.5 %collective-permute-start.4 = (f32[16,128]{1,0:T(8,128)S(1)}, f32[16,128]{1,0:T(8,128)S(1)}, u32[]{:S(2)}, u32[]{:S(2)}) collective-permute-start(f32[16,128]{1,0:T(8,128)S(1)} %add.15), channel_id=1, source_target_pairs={{0,4},{2,6},{4,0},{6,2},{8,12},{10,14},{12,8},{14,10},{16,20},{18,... | collective-permute-start | bytes 24584 | tf_op jit(solution)/shard_map/ppermute | solution.py:408
  39.4 2.2 %collective-permute-done.4 = f32[16,128]{1,0:T(8,128)S(1)} collective-permute-done((f32[16,128]{1,0:T(8,128)S(1)}, f32[16,128]{1,0:T(8,128)S(1)}, u32[]{:S(2)}, u32[]{:S(2)}) %collective-permute-start.4) | collective-permute-done | bytes 8224 | tf_op jit(solution)/shard_map/ppermute | solution.py:408
  41.5 1.6 %collective-permute-start.5 = (f32[16,128]{1,0:T(8,128)S(1)}, f32[16,128]{1,0:T(8,128)S(1)}, u32[]{:S(2)}, u32[]{:S(2)}) collective-permute-start(f32[16,128]{1,0:T(8,128)S(1)} %add.16), channel_id=1, source_target_pairs={{0,8},{2,10},{4,12},{6,14},{8,0},{10,2},{12,4},{14,6},{16,24},{18,... | collective-permute-start | bytes 24584 | tf_op jit(solution)/shard_map/ppermute | solution.py:408
  43.1 2.1 %collective-permute-done.5 = f32[16,128]{1,0:T(8,128)S(1)} collective-permute-done((f32[16,128]{1,0:T(8,128)S(1)}, f32[16,128]{1,0:T(8,128)S(1)}, u32[]{:S(2)}, u32[]{:S(2)}) %collective-permute-start.5) | collective-permute-done | bytes 8224 | tf_op jit(solution)/shard_map/ppermute | solution.py:408
  45.2 2.6 %collective-permute-start.6 = (f32[16,128]{1,0:T(8,128)S(1)}, f32[16,128]{1,0:T(8,128)S(1)}, u32[]{:S(2)}, u32[]{:S(2)}) collective-permute-start(f32[16,128]{1,0:T(8,128)S(1)} %add.17), channel_id=1, source_target_pairs={{0,16},{2,18},{4,20},{6,22},{8,24},{10,26},{12,28},{14,30},{16,0},... | collective-permute-start | bytes 24584 | tf_op jit(solution)/shard_map/ppermute | solution.py:408
  47.8 2.0 %collective-permute-done.6 = f32[16,128]{1,0:T(8,128)S(1)} collective-permute-done((f32[16,128]{1,0:T(8,128)S(1)}, f32[16,128]{1,0:T(8,128)S(1)}, u32[]{:S(2)}, u32[]{:S(2)}) %collective-permute-start.6) | collective-permute-done | bytes 8224 | tf_op jit(solution)/shard_map/ppermute | solution.py:408
  49.7 0.0 collective-permute-start.7
  49.7 3.6 %collective-permute-done.7 = f32[16,128]{1,0:T(8,128)S(1)} collective-permute-done((f32[16,128]{1,0:T(8,128)S(1)}, f32[16,128]{1,0:T(8,128)S(1)}, u32[]{:S(2)}, u32[]{:S(2)}) %collective-permute-start.7) | collective-permute-done | bytes 8224 | tf_op jit(solution)/shard_map/ppermute | solution.py:408
  53.4 0.6 %add.19.sums = f32[16,128]{1,0:T(8,128)} add(f32[16,128]{1,0:T(8,128)S(1)} %add.18, f32[16,128]{1,0:T(8,128)S(1)} %collective-permute-done.7) | non-fusion elementwise | flops 2048 | bytes 24576 | tf_op jit(solution)/shard_map/add | solution.py:408
  54.0 0.7 %copy-done.2 = f32[4,2,64,128]{3,2,1,0:T(8,128)} copy-done((f32[4,2,64,128]{3,2,1,0:T(8,128)}, f32[4,2,64,128]{3,2,1,0:T(8,128)S(1)}, u32[]{:S(2)}) %copy-start.2) | copy-done | bytes 262168
  54.7 2.0 %final.1 = (f32[2,64,256]{2,1,0:T(8,128)}, f32[2,64,256]{2,1,0:T(8,128)}) custom-call(f32[16,128]{1,0:T(8,128)} %add.19.sums, f32[4,2,64,128]{3,2,1,0:T(8,128)} %copy-done.1, f32[4,2,64,128]{3,2,1,0:T(8,128)} %copy-done.2, f32[2,64,256]{2,1,0:T(8,128)} %field.3), custom_call_target="tpu_custom_call" | custom-call | tf_op jit(solution)/shard_map/final/pallas_call | solution.py:412
  (8 shorter events, 0.0 us)
Async XLA Ops:
  2.8 14.9 %collective-permute-start = (f32[2,192,256]{2,1,0:T(8,128)}, f32[2,192,256]{2,1,0:T(8,128)S(1)}, u32[]{:S(2)}, u32[]{:S(2)}) collective-permute-start(f32[2,192,256]{2,1,0:T(8,128)} %get-tuple-element.8.refs_0_), channel_id=1, source_target_pairs={{0,1},{1,0},{2,3},{3,2},{4,5},{5,4},{6,7},{7,6},{8,9},{9,8},{10,11... | collective-permute-start | bytes 1179656 | tf_op jit(solution)/shard_map/ppermute | solution.py:355
  5.7 2.7 %collective-permute-start.1 = (f32[192,256]{1,0:T(8,128)}, f32[192,256]{1,0:T(8,128)S(1)}, u32[]{:S(2)}, u32[]{:S(2)}) collective-permute-start(f32[192,256]{1,0:T(8,128)} %get-tuple-element.9), channel_id=1, source_target_pairs={{0,2},{2,4},{3,1},{4,6},{5,3},{6,8},{7,5},{8,10},{9,7},{10,12},{11... | collective-permute-start | bytes 589832 | tf_op jit(solution)/shard_map/ppermute | solution.py:355
  7.2 1.3 %collective-permute-start.2 = (f32[192,256]{1,0:T(8,128)}, f32[192,256]{1,0:T(8,128)S(1)}, u32[]{:S(2)}, u32[]{:S(2)}) collective-permute-start(f32[192,256]{1,0:T(8,128)} %get-tuple-element.10), channel_id=1, source_target_pairs={{1,2},{2,1},{3,4},{4,3},{5,6},{6,5},{7,8},{8,7},{9,10},{10,9},{11,... | collective-permute-start | bytes 589832 | tf_op jit(solution)/shard_map/ppermute | solution.py:355
  17.7 1.0 %copy-start = (f32[2,192,256]{2,1,0:T(8,128)S(1)}, f32[2,192,256]{2,1,0:T(8,128)}, u32[]{:S(2)}) copy-start(f32[2,192,256]{2,1,0:T(8,128)} %get-tuple-element.8.refs_0_) | copy-start | bytes 1179652
  32.7 0.7 %copy-start.1 = (f32[4,2,64,128]{3,2,1,0:T(8,128)}, f32[4,2,64,128]{3,2,1,0:T(8,128)S(1)}, u32[]{:S(2)}) copy-start(f32[4,2,64,128]{3,2,1,0:T(8,128)S(1)} %get-tuple-element.12.mine) | copy-start | bytes 786436
  33.4 20.6 %collective-permute-start.8 = (f32[4,2,64,128]{3,2,1,0:T(8,128)S(1)}, f32[4,2,64,128]{3,2,1,0:T(8,128)S(1)}, u32[]{:S(2)}, u32[]{:S(2)}) collective-permute-start(f32[4,2,64,128]{3,2,1,0:T(8,128)S(1)} %get-tuple-element.13), channel_id=1, source_target_pairs={{0,1},{1,0},{2,3},{3,2},{4,5},{5,4},{6,7},{7,6},{8,9},{9,8},{10,11... | collective-permute-start | bytes 786440 | tf_op jit(solution)/shard_map/ppermute | solution.py:355
  36.7 1.2 %collective-permute-start.3 = (f32[16,128]{1,0:T(8,128)S(1)}, f32[16,128]{1,0:T(8,128)S(1)}, u32[]{:S(2)}, u32[]{:S(2)}) collective-permute-start(f32[16,128]{1,0:T(8,128)S(1)} %get-tuple-element.11), channel_id=1, source_target_pairs={{0,2},{2,0},{4,6},{6,4},{8,10},{10,8},{12,14},{14,12},{16,18},{18,... | collective-permute-start | bytes 24584 | tf_op jit(solution)/shard_map/ppermute | solution.py:408
  37.9 3.7 %collective-permute-start.4 = (f32[16,128]{1,0:T(8,128)S(1)}, f32[16,128]{1,0:T(8,128)S(1)}, u32[]{:S(2)}, u32[]{:S(2)}) collective-permute-start(f32[16,128]{1,0:T(8,128)S(1)} %add.15), channel_id=1, source_target_pairs={{0,4},{2,6},{4,0},{6,2},{8,12},{10,14},{12,8},{14,10},{16,20},{18,... | collective-permute-start | bytes 24584 | tf_op jit(solution)/shard_map/ppermute | solution.py:408
  41.5 3.7 %collective-permute-start.5 = (f32[16,128]{1,0:T(8,128)S(1)}, f32[16,128]{1,0:T(8,128)S(1)}, u32[]{:S(2)}, u32[]{:S(2)}) collective-permute-start(f32[16,128]{1,0:T(8,128)S(1)} %add.16), channel_id=1, source_target_pairs={{0,8},{2,10},{4,12},{6,14},{8,0},{10,2},{12,4},{14,6},{16,24},{18,... | collective-permute-start | bytes 24584 | tf_op jit(solution)/shard_map/ppermute | solution.py:408
  45.2 4.5 %collective-permute-start.6 = (f32[16,128]{1,0:T(8,128)S(1)}, f32[16,128]{1,0:T(8,128)S(1)}, u32[]{:S(2)}, u32[]{:S(2)}) collective-permute-start(f32[16,128]{1,0:T(8,128)S(1)} %add.17), channel_id=1, source_target_pairs={{0,16},{2,18},{4,20},{6,22},{8,24},{10,26},{12,28},{14,30},{16,0},... | collective-permute-start | bytes 24584 | tf_op jit(solution)/shard_map/ppermute | solution.py:408
  49.7 3.7 %collective-permute-start.7 = (f32[16,128]{1,0:T(8,128)S(1)}, f32[16,128]{1,0:T(8,128)S(1)}, u32[]{:S(2)}, u32[]{:S(2)}) collective-permute-start(f32[16,128]{1,0:T(8,128)S(1)} %add.18), channel_id=1, source_target_pairs={{0,1},{1,0},{2,3},{3,2},{4,5},{5,4},{6,7},{7,6},{8,9},{9,8},{10,11... | collective-permute-start | bytes 24584 | tf_op jit(solution)/shard_map/ppermute | solution.py:408
  54.0 0.7 %copy-start.2 = (f32[4,2,64,128]{3,2,1,0:T(8,128)}, f32[4,2,64,128]{3,2,1,0:T(8,128)S(1)}, u32[]{:S(2)}) copy-start(f32[4,2,64,128]{3,2,1,0:T(8,128)S(1)} %collective-permute-done.8.other) | copy-start | bytes 786436
where the time goes:
time: 56.9 us; the launch traced here: 56.7 us
  waiting for transfers between devices  20.8 us (37%)
  Pallas kernels  18.1 us (32%)
  starting transfers between devices  14.1 us (25%)
  local copies, waits for them, and re-layouts  2.38 us (4%)
  between operations  0.68 us (1%)
  other arithmetic  0.6 us (1%)
    pallas_call x1, Pallas kernels, shards(): pl.pallas_call(lambda *refs: window_kernel(pairs, *refs), out_shape=(part...  14 us
    ppermute x5, waiting for transfers between devices, shards(): lax.ppermute(sums, axis, [(at, at ^ hop) for at in range(size)])  11 us
    ppermute x4, waiting for transfers between devices, shifted(): return lax.ppermute(value, axes, perm)  9.8 us
    ppermute x4, starting transfers between devices, shifted(): return lax.ppermute(value, axes, perm)  8.43 us
    ppermute x5, starting transfers between devices, shards(): lax.ppermute(sums, axis, [(at, at ^ hop) for at in range(size)])  5.66 us
    unnamed x6, local copies, waits for them, and re-layouts  2.38 us
    pallas_call x1, Pallas kernels, shards(): pl.pallas_call(pack_kernel, out_shape=(jax.ShapeDtypeStruct((2, HALF_ROWS...  2.12 us
    pallas_call x1, Pallas kernels, shards(): pl.pallas_call(final_kernel, out_shape=(out, out), in_specs=[vmem] * 4, o...  1.98 us
  transfers between devices with their start and end apart: 9, of which 7 were waited for; matrix products, arithmetic and copies ran while one was open for 1% of the time, Pallas kernels for 0%

commit v1 on v0

v1 whole, which is shorter than its diff:
```python
import jax
import jax.numpy as jnp
from jax import lax
from jax.experimental import pallas as pl
from jax.experimental.pallas import tpu as pltpu
from jax.sharding import PartitionSpec as P

GRID = 32
BAND = 4
ITERS = 3
BEND_WEIGHT = 0.05
DAMPING = 0.5

SAMPLES = 256
LANES = 128
PACK = LANES // GRID
TILE_ROWS = 2
HALF_COLS = 4
PIECES = 3
WINDOW_COLS = PIECES * HALF_COLS
WIDTH = WINDOW_COLS * GRID
BLOCK_ROWS = TILE_ROWS * GRID
MASK_ROWS = 8
MASK_LANES = SAMPLES // HALF_COLS
TABLE_ROWS = 24
TABLES = BLOCK_ROWS + MASK_ROWS
HALF_ROWS = TABLES + HALF_COLS * TABLE_ROWS
BOUNDS = WINDOW_COLS - 1

LOW, HIGH = 0.5, 6.0
CENTRE, RADIUS = (HIGH + LOW) / 2, (HIGH - LOW) / 2

BASIS = ITERS + 1
PAIRS = [(i, j) for i in range(BASIS) for j in range(i, BASIS)]
SUM_ROWS = 16
SUM_LANES = LANES // SUM_ROWS
EDGE = 8

F32, BF16 = jnp.float32, jnp.bfloat16


def hat(offset):
    return jnp.maximum(1.0 - jnp.abs(offset), 0.0)


def pack_kernel(adjacency, field, target, rows, band, frac, own, ahead, back):
    part = lax.axis_index("row") % 2
    not_last_col = (lax.axis_index("col") < lax.axis_size("col") - 1).astype(jnp.int32)
    not_last_row = (lax.axis_index("row") < lax.axis_size("row") - 1).astype(jnp.int32)
    tiles = 2 * HALF_COLS
    sub = lax.broadcasted_iota(jnp.int32, (MASK_ROWS, SAMPLES), 0)
    for half in range(2):
        for comp in range(2):
            own[half, :BLOCK_ROWS, comp * LANES : (comp + 1) * LANES] = field[
                comp, :, half * LANES : (half + 1) * LANES
            ]
    for facing in range(4):
        along = rows[facing].astype(F32) + (frac[facing, 0].astype(F32) + 0.5) / 256.0
        across = band[facing].astype(F32) + (frac[facing, 1].astype(F32) + 0.5) / 256.0
        for tile in range(tiles):
            half, base = tile // HALF_COLS, TABLES + tile % HALF_COLS * TABLE_ROWS + 2 * facing
            lanes = slice(tile * SAMPLES, (tile + 1) * SAMPLES)
            own[half, base : base + 2, :] = along[:, lanes]
            own[half, base + 8 : base + 10, :] = across[:, lanes]
            own[half, base + 16 : base + 18, :] = target[facing // 2, facing % 2][:, lanes]
    unit = lax.broadcasted_iota(jnp.int32, (MASK_ROWS, SAMPLES), 1) // MASK_LANES
    for half in range(2):
        masks = jnp.zeros((MASK_ROWS, SAMPLES), F32)
        for tile in range(half * HALF_COLS, (half + 1) * HALF_COLS):
            for side in range(2):
                for row in range(TILE_ROWS):
                    value = adjacency[side, row, tile]
                    if side == 0 and tile == tiles - 1:
                        value = value * not_last_col
                    if side == 1 and row == TILE_ROWS - 1:
                        value = value * not_last_row
                    here = (sub == 2 * side + row) & (unit == tile % HALF_COLS)
                    masks = jnp.where(here, value.astype(F32), masks)
        own[half, BLOCK_ROWS:TABLES, :] = masks
    ahead[...] = own[1 - part]
    back[...] = own[part]


def split(value):
    high = value.astype(BF16)
    return high, (value - high.astype(F32)).astype(BF16)


def groups_of(pairs):
    order, counts = [], []
    for reach in range(ITERS + 1):
        step = ITERS - reach
        for bound in range(step, BOUNDS - step):
            order += [(0, bound, group) for group in range(pairs)]
        for piece in (1,) if step == ITERS else range(PIECES):
            order += [(1, row, piece) for row in range(4 * pairs - 1)]
        order = list(dict.fromkeys(order))
        counts.append(len(order))
    return order, counts[::-1]


def window_kernel(pairs, *refs):
    count = 4 * pairs
    pieces = refs[:count]
    mine, theirs, sums, slots, vecs, weight_hi, weight_lo, turned_hi, turned_lo, cross, shift, *rest = refs[count:]
    strip_in, strip_out, flipped, spread, bends, sems = rest
    order, counts = groups_of(pairs)
    own_pair = pairs // 2
    part = lax.axis_index("row") % 2

    copies = []
    for pair in range(pairs):
        places = (
            slots.at[2 * pair + part, pl.ds(1 - part, 2)],
            slots.at[2 * pair + 1 - part, pl.ds(1 - part, 2)],
            slots.at[2 * pair + part, 2 * part],
            slots.at[2 * pair + 1 - part, 2 * part],
        )
        for kind in range(4):
            at = 4 * pair + kind
            copies.append(pltpu.make_async_copy(pieces[at], places[kind], sems.at[at]))
    for copy in copies:
        copy.start()
    for copy in copies:
        copy.wait()

    sub8 = lax.broadcasted_iota(jnp.int32, (8, LANES), 0)
    lane8 = lax.broadcasted_iota(jnp.int32, (8, LANES), 1)
    near_side = sub8 >= 4
    sub16 = lax.broadcasted_iota(jnp.int32, (16, 2 * LANES), 0)
    lane16 = lax.broadcasted_iota(jnp.int32, (16, 2 * LANES), 1)
    side16 = (lane16 < LANES) == (sub16 % 8 >= 4)
    keep = [
        jnp.where(side16 & (lane16 % LANES // GRID == unit), 1.0, 0.0).astype(BF16)
        for unit in range(PACK)
    ]

    for block in range(2 * pairs):
        for piece in range(PIECES):
            for comp in range(2):
                start = EDGE + block * BLOCK_ROWS
                vecs[0, comp, piece, start : start + BLOCK_ROWS, :] = slots[
                    block, piece, :BLOCK_ROWS, comp * LANES : (comp + 1) * LANES
                ]

    def table(row, col, entry):
        start = TABLES + col % HALF_COLS * TABLE_ROWS + entry
        return slots[row // TILE_ROWS, col // HALF_COLS, start : start + 1, :]

    along_iota = lax.broadcasted_iota(jnp.int32, (GRID, SAMPLES), 0).astype(F32)
    sub_s = lax.broadcasted_iota(jnp.int32, (8, SAMPLES), 0)
    near_s = sub_s >= 4
    depth = jnp.where(near_s, 7 - sub_s, sub_s).astype(F32)

    def set_tables(index, direction, near_tiles, far_tiles):
        hats = []
        for unit in range(PACK):
            both = (near_tiles[unit], far_tiles[unit])
            ys = []
            for side in range(2):
                row, col = both[side]
                entry = 2 * (2 * direction + side) + row % TILE_ROWS
                weight = hat(table(row, col, entry) - along_iota)
                high, low = split(weight)
                start = side * LANES + unit * GRID
                weight_hi[index, start : start + GRID, :] = high
                weight_lo[index, start : start + GRID, :] = low
                hats.append(weight)
                ys.append(table(row, col, 8 + entry))
            row, col = both[0]
            at, lane = BLOCK_ROWS + 2 * direction + row % TILE_ROWS, col % HALF_COLS * MASK_LANES
            mask = slots[row // TILE_ROWS, col // HALF_COLS, at : at + 1, lane : lane + 1]
            signed = jnp.where(near_s, mask, -mask)
            rows = slice(8 * unit, 8 * unit + 8)
            across = hat(jnp.where(near_s, ys[0], ys[1]) - depth) * signed
            cross[index, rows, :] = across
            for comp in range(2):
                shift[index, 2 * unit + comp : 2 * unit + comp + 1, :] = table(
                    row, col, 16 + 4 * direction + 2 * comp + row % TILE_ROWS
                )
        ordered = jnp.concatenate(hats[0::2] + hats[1::2], axis=0).T
        high, low = split(ordered)
        turned_hi[index] = high
        turned_lo[index] = low

    for index, (direction, at, group) in enumerate(order):
        if direction == 0:
            tiles = [(PACK * group + unit, at) for unit in range(PACK)]
            set_tables(index, 0, tiles, [(row, col + 1) for row, col in tiles])
        else:
            tiles = [(at, PACK * group + unit) for unit in range(PACK)]
            set_tables(index, 1, tiles, [(row + 1, col) for row, col in tiles])

    spread[...] = jnp.zeros_like(spread)
    bends[...] = jnp.zeros_like(bends)

    def seam_batch(indices, first):
        half = 8 * 2 * PACK
        gathered = []
        for index in indices:
            high, low = split(jnp.concatenate([strip_in[index, comp] for comp in range(2)], axis=0))
            high = jnp.concatenate([high, high], axis=1)
            low = jnp.concatenate([low, low], axis=1)
            left = jnp.concatenate([high * keep[unit] for unit in range(PACK)] + [low * keep[unit] for unit in range(PACK)], axis=0)
            both = jnp.dot(left, weight_hi[index], preferred_element_type=F32)
            rest = jnp.dot(left[:half], weight_lo[index], preferred_element_type=F32)
            gathered.append(both[:half] + both[half:] + rest)
        pulled = []
        for index, values in zip(indices, gathered):
            parts = []
            for unit in range(PACK):
                across = cross[index, 8 * unit : 8 * unit + 8, :]
                for comp in range(2):
                    at = 2 * unit + comp
                    total = jnp.sum(values[8 * at : 8 * at + 8] * across, axis=0, keepdims=True)
                    if first:
                        total = total - shift[index, at : at + 1, :]
                    parts.append(total * across)
            pulled.append(split(jnp.concatenate(parts, axis=0)))
        numbers = (((1,), (0,)), ((), ()))
        backs = []
        for index, (high, low) in zip(indices, pulled):
            both = lax.dot_general(
                jnp.concatenate([high, low], axis=0), turned_hi[index], numbers, preferred_element_type=F32
            )
            rest = lax.dot_general(high, turned_lo[index], numbers, preferred_element_type=F32)
            backs.append(both[:half] + both[half:] + rest)
        for index, back in zip(indices, backs):
            for comp in range(2):
                out = None
                for unit in range(PACK):
                    at = 8 * (2 * unit + comp)
                    chosen = jnp.where(near_side, back[at : at + 8, :LANES], back[at : at + 8, LANES:])
                    out = chosen if out is None else jnp.where(lane8 // GRID == unit, chosen, out)
                strip_out[index, comp] = out

    sub32 = lax.broadcasted_iota(jnp.int32, (GRID, LANES), 0)
    lane32 = lax.broadcasted_iota(jnp.int32, (GRID, LANES), 1) % GRID
    inner = (sub32 >= 1) & (sub32 <= GRID - 2) & (lane32 >= 1) & (lane32 <= GRID - 2)

    def beside(value):
        return pltpu.roll(value, 1, 1) + pltpu.roll(value, LANES - 1, 1) - 4.0 * value

    def apply(step, scale, own_weight, last_weight):
        for comp in range(2):
            for group in range(pairs):
                for piece in range(PIECES):
                    start = EDGE + group * LANES
                    flipped[comp, piece * LANES : (piece + 1) * LANES, group * LANES : (group + 1) * LANES] = vecs[
                        step, comp, piece, start : start + LANES, :
                    ].T
        used = order[: counts[step]]

        def place(entry):
            direction, at, group = entry
            return GRID * at + GRID - 8, group, slice(group * LANES, (group + 1) * LANES), direction == 0

        for index, entry in enumerate(used):
            at, piece, lanes, east = place(entry)
            for comp in range(2):
                if east:
                    before, after = flipped[comp, at : at + 8, lanes], flipped[comp, at + 8 : at + 16, lanes]
                else:
                    start = EDGE + at
                    before = vecs[step, comp, piece, start : start + 8, :]
                    after = vecs[step, comp, piece, start + 8 : start + 16, :]
                strip_in[index, comp] = jnp.where(near_side, before, after)

        seam_batch(list(range(len(used))), step == 0)

        for index, entry in enumerate(used):
            at, piece, lanes, east = place(entry)
            if east:
                for comp in range(2):
                    spread[comp, at : at + 8, lanes] = jnp.where(near_side, strip_out[index, comp], 0.0)
                    spread[comp, at + 8 : at + 16, lanes] = jnp.where(near_side, 0.0, strip_out[index, comp])
        for piece in (1,) if step == ITERS else range(PIECES):
            for comp in range(2):
                for group in range(pairs):
                    turned = spread[
                        comp, piece * LANES : (piece + 1) * LANES, group * LANES : (group + 1) * LANES
                    ].T
                    for unit in range(PACK):
                        tile = PACK * group + unit
                        start = EDGE + tile * GRID
                        value = vecs[step, comp, piece, start : start + GRID, :]
                        level = jnp.where(
                            inner,
                            vecs[step, comp, piece, start - 1 : start + GRID - 1, :]
                            + vecs[step, comp, piece, start + 1 : start + GRID + 1, :]
                            + beside(value),
                            0.0,
                        )
                        bends[comp, piece, tile, EDGE : EDGE + GRID, :] = level
                        curved = (
                            bends[comp, piece, tile, EDGE - 1 : EDGE + GRID - 1, :]
                            + bends[comp, piece, tile, EDGE + 1 : EDGE + GRID + 1, :]
                            + beside(level)
                        )
                        out = scale * (turned[unit * GRID : (unit + 1) * GRID] + BEND_WEIGHT * curved)
                        if own_weight:
                            out = out + own_weight * value
                        if last_weight:
                            out = out + last_weight * vecs[step - 1, comp, piece, start : start + GRID, :]
                        vecs[step + 1, comp, piece, start : start + GRID, :] = out
        for index, entry in enumerate(used):
            at, piece, lanes, east = place(entry)
            if not east:
                start = EDGE + at
                for comp in range(2):
                    result = scale * strip_out[index, comp]
                    vecs[step + 1, comp, piece, start : start + 8, :] += jnp.where(near_side, result, 0.0)
                    vecs[step + 1, comp, piece, start + 8 : start + 16, :] += jnp.where(near_side, 0.0, result)

    apply(0, -1.0, 0.0, 0.0)
    apply(1, 1.0 / RADIUS, (DAMPING - CENTRE) / RADIUS, 0.0)
    apply(2, 2.0 / RADIUS, 2.0 * (DAMPING - CENTRE) / RADIUS, -1.0)
    apply(3, 2.0 / RADIUS, 2.0 * (DAMPING - CENTRE) / RADIUS, -1.0)

    first_row = EDGE + own_pair * 2 * BLOCK_ROWS
    partial = [jnp.zeros((8, LANES), F32) for _ in PAIRS]
    for comp in range(2):
        for row in range(first_row, first_row + 2 * BLOCK_ROWS, 8):
            values = [vecs[1 + k, comp, 1, row : row + 8, :] for k in range(BASIS)]
            for n, (i, j) in enumerate(PAIRS):
                partial[n] = partial[n] + values[i] * values[j]
    rows = [jnp.sum(value, axis=0, keepdims=True) for value in partial]
    rows.append(jnp.zeros((SUM_ROWS - len(rows), LANES), F32))
    totals = jnp.sum(jnp.concatenate(rows, axis=0), axis=1, keepdims=True)
    slot = lax.broadcasted_iota(jnp.int32, (SUM_ROWS, LANES), 1) // SUM_LANES
    placed = jnp.where(slot == lax.broadcasted_iota(jnp.int32, (SUM_ROWS, LANES), 0), totals, 0.0)
    sums[...] = jnp.broadcast_to(jnp.sum(placed, axis=0, keepdims=True), sums.shape)
    for k in range(BASIS):
        for comp in range(2):
            for out, block in ((mine, part), (theirs, 1 - part)):
                start = pl.multiple_of(first_row + block * BLOCK_ROWS, EDGE)
                out[k, comp] = vecs[1 + k, comp, 1, pl.ds(start, BLOCK_ROWS), :]


def final_kernel(*refs):
    sources, (control, residual), (sums, mine, other, field, sems) = refs[:4], refs[4:6], refs[6:]
    copies = [
        pltpu.make_async_copy(source, target, sems.at[n])
        for n, (source, target) in enumerate(zip(sources, (sums, mine, other, field)))
    ]
    for copy in copies:
        copy.start()
    copies[0].wait()
    part = lax.axis_index("row") % 2
    totals = jnp.sum(sums[...], axis=0, keepdims=True)
    gram = {}
    for n, (i, j) in enumerate(PAIRS):
        gram[i, j] = gram[j, i] = jnp.broadcast_to(totals[:, n * SUM_LANES : n * SUM_LANES + 1], (1, LANES))

    def inner(left, right):
        return sum(
            left[i] * sum(gram[i, j] * right[j] for j in right) for i in left
        )

    def image(vec):
        out = {}

        def add(at, value):
            out[at] = out[at] + value if at in out else value

        for k, value in vec.items():
            add(k, CENTRE * value)
            if k == 0:
                add(1, RADIUS * value)
            else:
                add(k - 1, RADIUS / 2 * value)
                add(k + 1, RADIUS / 2 * value)
        return out

    one = jnp.ones((1, LANES), F32)
    resid, direction, update = {0: one}, {0: one}, {}
    norm = gram[0, 0]
    for iteration in range(ITERS):
        moved = image(direction)
        step = norm / inner(direction, moved)
        for k, value in direction.items():
            update[k] = update[k] + step * value if k in update else step * value
        resid = {k: (resid[k] if k in resid else 0.0) - step * value for k, value in moved.items()}
        if iteration < ITERS - 1:
            after = inner(resid, resid)
            ratio = after / norm
            direction = {k: value + ratio * direction[k] if k in direction else value for k, value in resid.items()}
            norm = after

    for copy in copies[1:]:
        copy.wait()
    for source, half in ((mine, part), (other, 1 - part)):
        lanes = pl.ds(pl.multiple_of(half * LANES, LANES), LANES)
        for comp in range(2):
            basis = [source[k, comp] for k in range(BASIS)]
            control[comp, :, lanes] = field[comp, :, lanes] + sum(update[k] * basis[k] for k in update)
            residual[comp, :, lanes] = sum(resid[k] * basis[k] for k in resid)


def shards(start_field, seam_target, seam_rows, seam_band, seam_frac, adjacency):
    row_count, col_count = lax.axis_size("row"), lax.axis_size("col")
    axes = ("col", "row")
    vmem = pl.BlockSpec(memory_space=pltpu.VMEM)
    anywhere = pl.BlockSpec(memory_space=pl.ANY)
    small = pltpu.CompilerParams(vmem_limit_bytes=4 * 1024 * 1024)

    def shifted(value, move):
        sources = [(col, row) for col in range(col_count) for row in range(row_count)]
        perm = []
        for col, row in sources:
            to_col, to_row = move(col, row)
            if 0 <= to_col < col_count and 0 <= to_row < row_count:
                perm.append((col * row_count + row, to_col * row_count + to_row))
        return lax.ppermute(value, axes, perm)

    half = jax.ShapeDtypeStruct((HALF_ROWS, SAMPLES), F32)
    own, ahead, back = pl.pallas_call(
        pack_kernel,
        out_shape=(jax.ShapeDtypeStruct((2, HALF_ROWS, SAMPLES), F32), half, half),
        in_specs=[pl.BlockSpec(memory_space=pltpu.SMEM)] + [vmem] * 5,
        out_specs=(vmem, vmem, vmem),
        name="pack",
    )(adjacency, start_field, seam_target, seam_rows, seam_band, seam_frac)

    outward = lambda row: 1 - 2 * (row % 2)
    pieces = (
        own,
        shifted(own, lambda col, row: (col, row ^ 1)),
        shifted(ahead, lambda col, row: (col + outward(row), row)),
        shifted(back, lambda col, row: (col - outward(row), row ^ 1)),
    )
    if row_count > 2:
        from_above = [shifted(piece, lambda col, row: (col, row + 2)) for piece in pieces]
        from_below = [shifted(piece, lambda col, row: (col, row - 2)) for piece in pieces]
        pieces = (*from_above, *pieces, *from_below)
    pairs = len(pieces) // 4
    groups = len(groups_of(pairs)[0])
    limit = pltpu.CompilerParams(vmem_limit_bytes=(groups * 11 // 20 + 8 * pairs + 1) * 1024 * 1024)

    part_shape = jax.ShapeDtypeStruct((BASIS, 2, BLOCK_ROWS, LANES), F32)
    mine, theirs, sums = pl.pallas_call(
        lambda *refs: window_kernel(pairs, *refs),
        out_shape=(part_shape, part_shape, jax.ShapeDtypeStruct((row_count * col_count, LANES), F32)),
        in_specs=[anywhere] * len(pieces),
        out_specs=(vmem, vmem, vmem),
        scratch_shapes=[
            pltpu.VMEM((2 * pairs, PIECES, HALF_ROWS, SAMPLES), F32),
            pltpu.VMEM((BASIS + 1, 2, PIECES, 4 * pairs * GRID + 2 * EDGE, LANES), F32),
            pltpu.VMEM((groups, 2 * LANES, SAMPLES), BF16),
            pltpu.VMEM((groups, 2 * LANES, SAMPLES), BF16),
            pltpu.VMEM((groups, SAMPLES, 2 * LANES), BF16),
            pltpu.VMEM((groups, SAMPLES, 2 * LANES), BF16),
            pltpu.VMEM((groups, 8 * PACK, SAMPLES), F32),
            pltpu.VMEM((groups, 2 * PACK, SAMPLES), F32),
            pltpu.VMEM((groups, 2, 8, LANES), F32),
            pltpu.VMEM((groups, 2, 8, LANES), F32),
            pltpu.VMEM((2, WIDTH, pairs * LANES), F32),
            pltpu.VMEM((2, WIDTH, pairs * LANES), F32),
            pltpu.VMEM((2, PIECES, 4 * pairs, GRID + 2 * EDGE, LANES), F32),
            pltpu.SemaphoreType.DMA((len(pieces),)),
        ],
        compiler_params=limit,
        name="window",
    )(*pieces)

    other = shifted(theirs, lambda col, row: (col, row ^ 1))
    sums = lax.all_to_all(sums, axes, 0, 0, tiled=True)

    out = jax.ShapeDtypeStruct(start_field.shape, F32)
    return pl.pallas_call(
        final_kernel,
        out_shape=(out, out),
        in_specs=[anywhere] * 4,
        out_specs=(vmem, vmem),
        scratch_shapes=[
            pltpu.VMEM(sums.shape, F32),
            pltpu.VMEM(mine.shape, F32),
            pltpu.VMEM(mine.shape, F32),
            pltpu.VMEM(start_field.shape, F32),
            pltpu.SemaphoreType.DMA((4,)),
        ],
        compiler_params=small,
        name="final",
    )(sums, mine, other, start_field)


def solution(mesh):
    placed = (
        P(None, "row", "col"),
        P(None, None, "row", "col"),
        P(None, "row", "col"),
        P(None, "row", "col"),
        P(None, None, "row", "col"),
        P(None, "row", "col"),
    )
    return jax.shard_map(
        shards,
        mesh=mesh,
        in_specs=placed,
        out_specs=(P(None, "row", "col"), P(None, "row", "col")),
        check_vma=False,
    )
```

time: 56.9 us -> 42.6 us (0.75)
  waiting for transfers between devices: 20.8 us -> 8.48 us
  blocking collectives: 0 us -> 11 us
  starting transfers between devices: 14.1 us -> 8.24 us
  Pallas kernels: 18.1 us -> 13.1 us
  local copies, waits for them, and re-layouts: 2.38 us -> 0.98 us
  other arithmetic: 0.6 us -> 0 us
    ppermute x5 -> x0, waiting for transfers between devices: 11 us -> none  [shards(): lax.ppermute(sums, axis, [(at, at ^ hop) for at in range(size)])]
    all_to_all x0 -> x1, blocking collectives: none -> 11 us  [shards(): sums = lax.all_to_all(sums, axes, 0, 0, tiled=True)]
    ppermute x5 -> x0, starting transfers between devices: 5.66 us -> none  [shards(): lax.ppermute(sums, axis, [(at, at ^ hop) for at in range(size)])]
    pallas_call x1, Pallas kernels: 14 us -> 9.8 us  [shards(): pl.pallas_call(lambda *refs: window_kernel(pairs, *refs), out_shape=(part...]
    unnamed x6 -> x4, local copies, waits for them, and re-layouts: 2.38 us -> 0.98 us
    ppermute x4, waiting for transfers between devices: 9.8 us -> 8.48 us  [shifted(): return lax.ppermute(value, axes, perm)]
    pallas_call x1, Pallas kernels: 1.98 us -> 1.16 us  [shards(): pl.pallas_call(final_kernel, out_shape=(out, out), in_specs=[anywhere] *...]
    add x5 -> x0, other arithmetic: 0.6 us -> none  [shards(): sums + lax.ppermute(sums, axis, [(at, at ^ hop) for at in range(size)])]
  transfers between devices with their start and end apart: 9 -> 4, of which waited for: 7 -> 2; matrix products, arithmetic and copies ran while one was open for 1% -> 0% of each run, Pallas kernels for 0% -> 0%
where the time goes in v1:
time: 42.6 us; the launch traced here: 42.4 us
  Pallas kernels  13.1 us (31%)
  blocking collectives  11 us (26%)
  waiting for transfers between devices  8.48 us (20%)
  starting transfers between devices  8.24 us (19%)
  local copies, waits for them, and re-layouts  0.98 us (2%)
  between operations  0.66 us (2%)
    all_to_all x1, blocking collectives, shards(): sums = lax.all_to_all(sums, axes, 0, 0, tiled=True)  11 us
    pallas_call x1, Pallas kernels, shards(): pl.pallas_call(lambda *refs: window_kernel(pairs, *refs), out_shape=(part...  9.8 us
    ppermute x4, waiting for transfers between devices, shifted(): return lax.ppermute(value, axes, perm)  8.48 us
    ppermute x4, starting transfers between devices, shifted(): return lax.ppermute(value, axes, perm)  8.24 us
    pallas_call x1, Pallas kernels, shards(): pl.pallas_call(pack_kernel, out_shape=(jax.ShapeDtypeStruct((2, HALF_ROWS...  2.09 us
    pallas_call x1, Pallas kernels, shards(): pl.pallas_call(final_kernel, out_shape=(out, out), in_specs=[anywhere] *...  1.16 us
    unnamed x4, local copies, waits for them, and re-layouts  0.98 us
  transfers between devices with their start and end apart: 4, of which 2 were waited for; matrix products, arithmetic and copies ran while one was open for 0% of the time, Pallas kernels for 0%

profile of v1, /device:TPU:0, one launch (start us, length us, event | category | flops | bytes accessed | tf_op | source)
XLA Modules:
  0.0 42.4 jit_solution(13433834176876199799)
XLA Ops:
  0.6 2.1 %pack.1 = (f32[2,168,256]{2,1,0:T(8,128)}, f32[168,256]{1,0:T(8,128)}, f32[168,256]{1,0:T(8,128)}) custom-call(s32[2,2,8]{2,1,0:T(2,128)} %adjacency.1, f32[2,64,256]{2,1,0:T(8,128)} %refs_3_.1, f32[2,2,2,2048]{3,2,1,0:T(2,128)} %target.1, s32[4,2,2048]{2,1,0:T(2,128)} %rows.1, s32[4,2,2048]{2,1,0:T(2,128)} %band.1, s32[4,2,2,2048]{3,2,1,0:T(2,128)} %frac.1), custom_call_target="tpu_custom_call" | custom-call | tf_op jit(solution)/shard_map/pack/pallas_call | solution.py:417
  2.7 3.0 %collective-permute-start = (f32[2,168,256]{2,1,0:T(8,128)}, f32[2,168,256]{2,1,0:T(8,128)S(1)}, u32[]{:S(2)}, u32[]{:S(2)}) collective-permute-start(f32[2,168,256]{2,1,0:T(8,128)} %get-tuple-element.8.refs_0_), channel_id=1, source_target_pairs={{0,1},{1,0},{2,3},{3,2},{4,5},{5,4},{6,7},{7,6},{8,9},{9,8},{10,11... | collective-permute-start | bytes 1032200 | tf_op jit(solution)/shard_map/ppermute | solution.py:414
  5.7 1.5 %collective-permute-start.1 = (f32[168,256]{1,0:T(8,128)}, f32[168,256]{1,0:T(8,128)S(1)}, u32[]{:S(2)}, u32[]{:S(2)}) collective-permute-start(f32[168,256]{1,0:T(8,128)} %get-tuple-element.9), channel_id=1, source_target_pairs={{0,2},{2,4},{3,1},{4,6},{5,3},{6,8},{7,5},{8,10},{9,7},{10,12},{11... | collective-permute-start | bytes 516104 | tf_op jit(solution)/shard_map/ppermute | solution.py:414
  7.2 0.7 %collective-permute-start.2 = (f32[168,256]{1,0:T(8,128)}, f32[168,256]{1,0:T(8,128)S(1)}, u32[]{:S(2)}, u32[]{:S(2)}) collective-permute-start(f32[168,256]{1,0:T(8,128)} %get-tuple-element.10), channel_id=1, source_target_pairs={{1,2},{2,1},{3,4},{4,3},{5,6},{6,5},{7,8},{8,7},{9,10},{10,9},{11,... | collective-permute-start | bytes 516104 | tf_op jit(solution)/shard_map/ppermute | solution.py:414
  7.8 0.5 %collective-permute-done.1.refs_2_ = f32[168,256]{1,0:T(8,128)S(1)} collective-permute-done((f32[168,256]{1,0:T(8,128)}, f32[168,256]{1,0:T(8,128)S(1)}, u32[]{:S(2)}, u32[]{:S(2)}) %collective-permute-start.1) | collective-permute-done | bytes 172064 | tf_op jit(solution)/shard_map/ppermute | solution.py:414
  8.4 0.0 collective-permute-done.2.refs_3_
  8.4 7.9 %collective-permute-done.refs_1_ = f32[2,168,256]{2,1,0:T(8,128)S(1)} collective-permute-done((f32[2,168,256]{2,1,0:T(8,128)}, f32[2,168,256]{2,1,0:T(8,128)S(1)}, u32[]{:S(2)}, u32[]{:S(2)}) %collective-permute-start) | collective-permute-done | bytes 344096 | tf_op jit(solution)/shard_map/ppermute | solution.py:414
  16.3 0.0 copy-start.1
  16.3 1.0 %copy-done.1 = f32[2,168,256]{2,1,0:T(8,128)S(1)} copy-done((f32[2,168,256]{2,1,0:T(8,128)S(1)}, f32[2,168,256]{2,1,0:T(8,128)}, u32[]{:S(2)}) %copy-start.1) | copy-done | bytes 344088
  17.3 0.0 copy-start
  17.3 9.8 %window.1 = (f32[4,2,64,128]{3,2,1,0:T(8,128)S(1)}, f32[4,2,64,128]{3,2,1,0:T(8,128)S(1)}, f32[32,128]{1,0:T(8,128)S(1)}) custom-call(f32[2,168,256]{2,1,0:T(8,128)S(1)} %copy-done.1, f32[2,168,256]{2,1,0:T(8,128)S(1)} %collective-permute-done.refs_1_, f32[168,256]{1,0:T(8,128)S(1)} %collective-permute-done.1.refs_2_, ...), custom_call_target="tpu_custom_call" | custom-call | tf_op jit(solution)/shard_map/window/pallas_call | solution.py:441
  27.1 3.1 %collective-permute-start.3 = (f32[4,2,64,128]{3,2,1,0:T(8,128)S(1)}, f32[4,2,64,128]{3,2,1,0:T(8,128)S(1)}, u32[]{:S(2)}, u32[]{:S(2)}) collective-permute-start(f32[4,2,64,128]{3,2,1,0:T(8,128)S(1)} %get-tuple-element.13), channel_id=1, source_target_pairs={{0,1},{1,0},{2,3},{3,2},{4,5},{5,4},{6,7},{7,6},{8,9},{9,8},{10,11... | collective-permute-start | bytes 786440 | tf_op jit(solution)/shard_map/ppermute | solution.py:414
  30.2 11.0 %all_to_all.11 = f32[32,1,128]{2,1,0:T(1,128)S(1)} all-to-all(f32[32,1,128]{2,1,0:T(1,128)S(1)} %bitcast.5), channel_id=1, replica_groups=mesh['col'=16,'row'=2] {'col','row'}, dimensions={0} | all-to-all | bytes 32768 | tf_op jit(solution)/shard_map/all_to_all | solution.py:467
  41.2 0.0 collective-permute-done.3.refs_2_
  41.2 0.0 copy-done
  41.2 1.2 %final.1 = (f32[2,64,256]{2,1,0:T(8,128)}, f32[2,64,256]{2,1,0:T(8,128)}) custom-call(f32[32,128]{1,0:T(8,128)S(1)} %bitcast.4, f32[4,2,64,128]{3,2,1,0:T(8,128)S(1)} %get-tuple-element.12.refs_1_, f32[4,2,64,128]{3,2,1,0:T(8,128)S(1)} %collective-permute-done.3.refs_2_, f32[2,64,256]{2,1,0:T(8,128)S(1)} %copy-done), custom_call_target="tpu_custom_call" | custom-call | tf_op jit(solution)/shard_map/final/pallas_call | solution.py:470
Async XLA Ops:
  2.7 13.6 %collective-permute-start = (f32[2,168,256]{2,1,0:T(8,128)}, f32[2,168,256]{2,1,0:T(8,128)S(1)}, u32[]{:S(2)}, u32[]{:S(2)}) collective-permute-start(f32[2,168,256]{2,1,0:T(8,128)} %get-tuple-element.8.refs_0_), channel_id=1, source_target_pairs={{0,1},{1,0},{2,3},{3,2},{4,5},{5,4},{6,7},{7,6},{8,9},{9,8},{10,11... | collective-permute-start | bytes 1032200 | tf_op jit(solution)/shard_map/ppermute | solution.py:414
  5.7 2.7 %collective-permute-start.1 = (f32[168,256]{1,0:T(8,128)}, f32[168,256]{1,0:T(8,128)S(1)}, u32[]{:S(2)}, u32[]{:S(2)}) collective-permute-start(f32[168,256]{1,0:T(8,128)} %get-tuple-element.9), channel_id=1, source_target_pairs={{0,2},{2,4},{3,1},{4,6},{5,3},{6,8},{7,5},{8,10},{9,7},{10,12},{11... | collective-permute-start | bytes 516104 | tf_op jit(solution)/shard_map/ppermute | solution.py:414
  7.2 1.2 %collective-permute-start.2 = (f32[168,256]{1,0:T(8,128)}, f32[168,256]{1,0:T(8,128)S(1)}, u32[]{:S(2)}, u32[]{:S(2)}) collective-permute-start(f32[168,256]{1,0:T(8,128)} %get-tuple-element.10), channel_id=1, source_target_pairs={{1,2},{2,1},{3,4},{4,3},{5,6},{6,5},{7,8},{8,7},{9,10},{10,9},{11,... | collective-permute-start | bytes 516104 | tf_op jit(solution)/shard_map/ppermute | solution.py:414
  16.3 1.0 %copy-start.1 = (f32[2,168,256]{2,1,0:T(8,128)S(1)}, f32[2,168,256]{2,1,0:T(8,128)}, u32[]{:S(2)}) copy-start(f32[2,168,256]{2,1,0:T(8,128)} %get-tuple-element.8.refs_0_) | copy-start | bytes 1032196
  17.3 23.9 %copy-start = (f32[2,64,256]{2,1,0:T(8,128)S(1)}, f32[2,64,256]{2,1,0:T(8,128)}, u32[]{:S(2)}) copy-start(f32[2,64,256]{2,1,0:T(8,128)} %refs_3_.1) | copy-start | bytes 393220
  27.1 14.1 %collective-permute-start.3 = (f32[4,2,64,128]{3,2,1,0:T(8,128)S(1)}, f32[4,2,64,128]{3,2,1,0:T(8,128)S(1)}, u32[]{:S(2)}, u32[]{:S(2)}) collective-permute-start(f32[4,2,64,128]{3,2,1,0:T(8,128)S(1)} %get-tuple-element.13), channel_id=1, source_target_pairs={{0,1},{1,0},{2,3},{3,2},{4,5},{5,4},{6,7},{7,6},{8,9},{9,8},{10,11... | collective-permute-start | bytes 786440 | tf_op jit(solution)/shard_map/ppermute | solution.py:414

commit v2 on v1

--- a/solution.py
+++ b/solution.py
@@ -21,7 +21,6 @@
 WIDTH = WINDOW_COLS * GRID
 BLOCK_ROWS = TILE_ROWS * GRID
 MASK_ROWS = 8
-MASK_LANES = SAMPLES // HALF_COLS
 TABLE_ROWS = 24
 TABLES = BLOCK_ROWS + MASK_ROWS
 HALF_ROWS = TABLES + HALF_COLS * TABLE_ROWS
@@ -43,7 +42,16 @@
     return jnp.maximum(1.0 - jnp.abs(offset), 0.0)
 
 
-def pack_kernel(adjacency, field, target, rows, band, frac, own, ahead, back):
+def pack_kernel(*refs):
+    sources, (own, ahead, back), (*copied, sems) = refs[:6], refs[6:9], refs[9:]
+    field, target, rows, band, frac, adjacency = copied
+    copies = [
+        pltpu.make_async_copy(source, place, sems.at[n]) for n, (source, place) in enumerate(zip(sources, copied))
+    ]
+    for copy in copies:
+        copy.start()
+    for copy in copies:
+        copy.wait()
     part = lax.axis_index("row") % 2
     not_last_col = (lax.axis_index("col") < lax.axis_size("col") - 1).astype(jnp.int32)
     not_last_row = (lax.axis_index("row") < lax.axis_size("row") - 1).astype(jnp.int32)
@@ -63,7 +71,7 @@
             own[half, base : base + 2, :] = along[:, lanes]
             own[half, base + 8 : base + 10, :] = across[:, lanes]
             own[half, base + 16 : base + 18, :] = target[facing // 2, facing % 2][:, lanes]
-    unit = lax.broadcasted_iota(jnp.int32, (MASK_ROWS, SAMPLES), 1) // MASK_LANES
+    place = 2 * sub + lax.broadcasted_iota(jnp.int32, (MASK_ROWS, SAMPLES), 1) // LANES
     for half in range(2):
         masks = jnp.zeros((MASK_ROWS, SAMPLES), F32)
         for tile in range(half * HALF_COLS, (half + 1) * HALF_COLS):
@@ -74,8 +82,8 @@
                         value = value * not_last_col
                     if side == 1 and row == TILE_ROWS - 1:
                         value = value * not_last_row
-                    here = (sub == 2 * side + row) & (unit == tile % HALF_COLS)
-                    masks = jnp.where(here, value.astype(F32), masks)
+                    entry = 4 * (tile % HALF_COLS) + 2 * side + row
+                    masks = jnp.where(place == entry, value.astype(F32), masks)
         own[half, BLOCK_ROWS:TABLES, :] = masks
     ahead[...] = own[1 - part]
     back[...] = own[part]
@@ -168,8 +176,10 @@
                 hats.append(weight)
                 ys.append(table(row, col, 8 + entry))
             row, col = both[0]
-            at, lane = BLOCK_ROWS + 2 * direction + row % TILE_ROWS, col % HALF_COLS * MASK_LANES
-            mask = slots[row // TILE_ROWS, col // HALF_COLS, at : at + 1, lane : lane + 1]
+            entry = 4 * (col % HALF_COLS) + 2 * direction + row % TILE_ROWS
+            at, lane = BLOCK_ROWS + entry // 2, entry % 2 * LANES
+            mask = slots[row // TILE_ROWS, col // HALF_COLS, at : at + 1, lane : lane + LANES]
+            mask = jnp.concatenate([mask, mask], axis=1)
             signed = jnp.where(near_s, mask, -mask)
             rows = slice(8 * unit, 8 * unit + 8)
             across = hat(jnp.where(near_s, ys[0], ys[1]) - depth) * signed
@@ -414,13 +424,17 @@
         return lax.ppermute(value, axes, perm)
 
     half = jax.ShapeDtypeStruct((HALF_ROWS, SAMPLES), F32)
+    inputs = (start_field, seam_target, seam_rows, seam_band, seam_frac, adjacency)
     own, ahead, back = pl.pallas_call(
         pack_kernel,
         out_shape=(jax.ShapeDtypeStruct((2, HALF_ROWS, SAMPLES), F32), half, half),
-        in_specs=[pl.BlockSpec(memory_space=pltpu.SMEM)] + [vmem] * 5,
+        in_specs=[anywhere] * 6,
         out_specs=(vmem, vmem, vmem),
+        scratch_shapes=[pltpu.VMEM(value.shape, value.dtype) for value in inputs[:5]]
+        + [pltpu.SMEM(adjacency.shape, adjacency.dtype), pltpu.SemaphoreType.DMA((6,))],
+        compiler_params=small,
         name="pack",
-    )(adjacency, start_field, seam_target, seam_rows, seam_band, seam_frac)
+    )(*(pltpu.with_memory_space_constraint(value, pltpu.HBM) for value in inputs))
 
     outward = lambda row: 1 - 2 * (row % 2)
     pieces = (

time: 42.6 us -> 39.9 us (0.937)
  Pallas kernels: 13.1 us -> 11.5 us
  local copies, waits for them, and re-layouts: 0.98 us -> 0.01 us
    unnamed x4 -> x2, local copies, waits for them, and re-layouts: 0.98 us -> 0.01 us
    pallas_call x1, Pallas kernels: 2.09 us -> 1.28 us  [shards(): pl.pallas_call(pack_kernel, out_shape=(jax.ShapeDtypeStruct((2, HALF_ROWS...]
    pallas_call x1, Pallas kernels: 9.8 us -> 9.02 us  [shards(): pl.pallas_call(lambda *refs: window_kernel(pairs, *refs), out_shape=(part...]
where the time goes in v2:
time: 39.9 us; the launch traced here: 39.7 us
  Pallas kernels  11.5 us (29%)
  blocking collectives  11 us (28%)
  starting transfers between devices  8.41 us (21%)
  waiting for transfers between devices  8.17 us (20%)
  between operations  0.67 us (2%)
    all_to_all x1, blocking collectives, shards(): sums = lax.all_to_all(sums, axes, 0, 0, tiled=True)  11 us
    pallas_call x1, Pallas kernels, shards(): pl.pallas_call(lambda *refs: window_kernel(pairs, *refs), out_shape=(part...  9.02 us
    ppermute x4, starting transfers between devices, shifted(): return lax.ppermute(value, axes, perm)  8.41 us
    ppermute x4, waiting for transfers between devices, shifted(): return lax.ppermute(value, axes, perm)  8.17 us
    pallas_call x1, Pallas kernels, shards(): pl.pallas_call(pack_kernel, out_shape=(jax.ShapeDtypeStruct((2, HALF_ROWS...  1.28 us
    pallas_call x1, Pallas kernels, shards(): pl.pallas_call(final_kernel, out_shape=(out, out), in_specs=[anywhere] *...  1.16 us
  transfers between devices with their start and end apart: 4, of which 2 were waited for; matrix products, arithmetic and copies ran while one was open for 0% of the time, Pallas kernels for 0%

profile of v2, /device:TPU:0, one launch (start us, length us, event | category | flops | bytes accessed | tf_op | source)
XLA Modules:
  0.0 39.7 jit_solution(542127263341138542)
XLA Ops:
  0.6 1.3 %pack.1 = (f32[2,168,256]{2,1,0:T(8,128)S(1)}, f32[168,256]{1,0:T(8,128)S(1)}, f32[168,256]{1,0:T(8,128)S(1)}) custom-call(f32[2,64,256]{2,1,0:T(8,128)} %refs_3_.3, f32[2,2,2,2048]{3,2,1,0:T(2,128)} %refs_1_.1, s32[4,2,2048]{2,1,0:T(2,128)} %refs_2_.1, s32[4,2,2048]{2,1,0:T(2,128)} %refs_3_.2, s32[4,2,2,2048]{3,2,1,0:T(2,128)} %refs_4_.1, s32[2,2,8]{2,1,0:T(2,128)} %refs_5_.1), custom_call_target="tpu_custom_call" | custom-call | tf_op jit(solution)/shard_map/pack/pallas_call | solution.py:428
  1.9 3.0 %collective-permute-start = (f32[2,168,256]{2,1,0:T(8,128)S(1)}, f32[2,168,256]{2,1,0:T(8,128)S(1)}, u32[]{:S(2)}, u32[]{:S(2)}) collective-permute-start(f32[2,168,256]{2,1,0:T(8,128)S(1)} %get-tuple-element.8.refs_0_), channel_id=1, source_target_pairs={{0,1},{1,0},{2,3},{3,2},{4,5},{5,4},{6,7},{7,6},{8,9},{9,8},{10,11... | collective-permute-start | bytes 1032200 | tf_op jit(solution)/shard_map/ppermute | solution.py:424
  4.9 1.5 %collective-permute-start.1 = (f32[168,256]{1,0:T(8,128)S(1)}, f32[168,256]{1,0:T(8,128)S(1)}, u32[]{:S(2)}, u32[]{:S(2)}) collective-permute-start(f32[168,256]{1,0:T(8,128)S(1)} %get-tuple-element.9), channel_id=1, source_target_pairs={{0,2},{2,4},{3,1},{4,6},{5,3},{6,8},{7,5},{8,10},{9,7},{10,12},{11... | collective-permute-start | bytes 516104 | tf_op jit(solution)/shard_map/ppermute | solution.py:424
  6.4 0.7 %collective-permute-start.2 = (f32[168,256]{1,0:T(8,128)S(1)}, f32[168,256]{1,0:T(8,128)S(1)}, u32[]{:S(2)}, u32[]{:S(2)}) collective-permute-start(f32[168,256]{1,0:T(8,128)S(1)} %get-tuple-element.10), channel_id=1, source_target_pairs={{1,2},{2,1},{3,4},{4,3},{5,6},{6,5},{7,8},{8,7},{9,10},{10,9},{11,... | collective-permute-start | bytes 516104 | tf_op jit(solution)/shard_map/ppermute | solution.py:424
  7.1 0.3 collective-permute-done.1.refs_2_
  7.4 0.0 collective-permute-done.2.refs_3_
  7.4 7.8 %collective-permute-done.refs_1_ = f32[2,168,256]{2,1,0:T(8,128)S(1)} collective-permute-done((f32[2,168,256]{2,1,0:T(8,128)S(1)}, f32[2,168,256]{2,1,0:T(8,128)S(1)}, u32[]{:S(2)}, u32[]{:S(2)}) %collective-permute-start) | collective-permute-done | bytes 344096 | tf_op jit(solution)/shard_map/ppermute | solution.py:424
  15.3 0.0 copy-start
  15.3 9.0 %window.1 = (f32[4,2,64,128]{3,2,1,0:T(8,128)S(1)}, f32[4,2,64,128]{3,2,1,0:T(8,128)S(1)}, f32[32,128]{1,0:T(8,128)S(1)}) custom-call(f32[2,168,256]{2,1,0:T(8,128)S(1)} %get-tuple-element.8.refs_0_, f32[2,168,256]{2,1,0:T(8,128)S(1)} %collective-permute-done.refs_1_, f32[168,256]{1,0:T(8,128)S(1)} %collective-permute-done.1.refs_2_, ...), custom_call_target="tpu_custom_call" | custom-call | tf_op jit(solution)/shard_map/window/pallas_call | solution.py:455
  24.3 3.3 %collective-permute-start.3 = (f32[4,2,64,128]{3,2,1,0:T(8,128)S(1)}, f32[4,2,64,128]{3,2,1,0:T(8,128)S(1)}, u32[]{:S(2)}, u32[]{:S(2)}) collective-permute-start(f32[4,2,64,128]{3,2,1,0:T(8,128)S(1)} %get-tuple-element.13), channel_id=1, source_target_pairs={{0,1},{1,0},{2,3},{3,2},{4,5},{5,4},{6,7},{7,6},{8,9},{9,8},{10,11... | collective-permute-start | bytes 786440 | tf_op jit(solution)/shard_map/ppermute | solution.py:424
  27.5 11.0 %all_to_all.11 = f32[32,1,128]{2,1,0:T(1,128)S(1)} all-to-all(f32[32,1,128]{2,1,0:T(1,128)S(1)} %bitcast.5), channel_id=1, replica_groups=mesh['col'=16,'row'=2] {'col','row'}, dimensions={0} | all-to-all | bytes 32768 | tf_op jit(solution)/shard_map/all_to_all | solution.py:481
  38.5 0.0 collective-permute-done.3.refs_2_
  38.5 0.0 copy-done
  38.5 1.2 %final.1 = (f32[2,64,256]{2,1,0:T(8,128)}, f32[2,64,256]{2,1,0:T(8,128)}) custom-call(f32[32,128]{1,0:T(8,128)S(1)} %bitcast.4, f32[4,2,64,128]{3,2,1,0:T(8,128)S(1)} %get-tuple-element.12.refs_1_, f32[4,2,64,128]{3,2,1,0:T(8,128)S(1)} %collective-permute-done.3.refs_2_, f32[2,64,256]{2,1,0:T(8,128)S(1)} %copy-done), custom_call_target="tpu_custom_call" | custom-call | tf_op jit(solution)/shard_map/final/pallas_call | solution.py:484
Async XLA Ops:
  1.9 13.3 %collective-permute-start = (f32[2,168,256]{2,1,0:T(8,128)S(1)}, f32[2,168,256]{2,1,0:T(8,128)S(1)}, u32[]{:S(2)}, u32[]{:S(2)}) collective-permute-start(f32[2,168,256]{2,1,0:T(8,128)S(1)} %get-tuple-element.8.refs_0_), channel_id=1, source_target_pairs={{0,1},{1,0},{2,3},{3,2},{4,5},{5,4},{6,7},{7,6},{8,9},{9,8},{10,11... | collective-permute-start | bytes 1032200 | tf_op jit(solution)/shard_map/ppermute | solution.py:424
  4.9 2.5 %collective-permute-start.1 = (f32[168,256]{1,0:T(8,128)S(1)}, f32[168,256]{1,0:T(8,128)S(1)}, u32[]{:S(2)}, u32[]{:S(2)}) collective-permute-start(f32[168,256]{1,0:T(8,128)S(1)} %get-tuple-element.9), channel_id=1, source_target_pairs={{0,2},{2,4},{3,1},{4,6},{5,3},{6,8},{7,5},{8,10},{9,7},{10,12},{11... | collective-permute-start | bytes 516104 | tf_op jit(solution)/shard_map/ppermute | solution.py:424
  6.4 1.0 %collective-permute-start.2 = (f32[168,256]{1,0:T(8,128)S(1)}, f32[168,256]{1,0:T(8,128)S(1)}, u32[]{:S(2)}, u32[]{:S(2)}) collective-permute-start(f32[168,256]{1,0:T(8,128)S(1)} %get-tuple-element.10), channel_id=1, source_target_pairs={{1,2},{2,1},{3,4},{4,3},{5,6},{6,5},{7,8},{8,7},{9,10},{10,9},{11,... | collective-permute-start | bytes 516104 | tf_op jit(solution)/shard_map/ppermute | solution.py:424
  15.3 23.3 %copy-start = (f32[2,64,256]{2,1,0:T(8,128)S(1)}, f32[2,64,256]{2,1,0:T(8,128)}, u32[]{:S(2)}) copy-start(f32[2,64,256]{2,1,0:T(8,128)} %refs_3_.3) | copy-start | bytes 393220
  24.3 14.2 %collective-permute-start.3 = (f32[4,2,64,128]{3,2,1,0:T(8,128)S(1)}, f32[4,2,64,128]{3,2,1,0:T(8,128)S(1)}, u32[]{:S(2)}, u32[]{:S(2)}) collective-permute-start(f32[4,2,64,128]{3,2,1,0:T(8,128)S(1)} %get-tuple-element.13), channel_id=1, source_target_pairs={{0,1},{1,0},{2,3},{3,2},{4,5},{5,4},{6,7},{7,6},{8,9},{9,8},{10,11... | collective-permute-start | bytes 786440 | tf_op jit(solution)/shard_map/ppermute | solution.py:424

commit v3 on v2

--- a/solution.py
+++ b/solution.py
@@ -25,6 +25,7 @@
 TABLES = BLOCK_ROWS + MASK_ROWS
 HALF_ROWS = TABLES + HALF_COLS * TABLE_ROWS
 BOUNDS = WINDOW_COLS - 1
+PLACED = ((0, 1, 10, 11), (4, 5, 6, 7), (8, 9, 2, 3))
 
 LOW, HIGH = 0.5, 6.0
 CENTRE, RADIUS = (HIGH + LOW) / 2, (HIGH - LOW) / 2
@@ -94,13 +95,23 @@
     return high, (value - high.astype(F32)).astype(BF16)
 
 
+def position(col):
+    for piece, cols in enumerate(PLACED):
+        if col in cols:
+            return piece * LANES + cols.index(col) * GRID
+
+
+def pieces_at(step):
+    return ((1, 2, 0), (1, 2), (1, 2), (1,))[step]
+
+
 def groups_of(pairs):
     order, counts = [], []
     for reach in range(ITERS + 1):
         step = ITERS - reach
         for bound in range(step, BOUNDS - step):
             order += [(0, bound, group) for group in range(pairs)]
-        for piece in (1,) if step == ITERS else range(PIECES):
+        for piece in pieces_at(step):
             order += [(1, row, piece) for row in range(4 * pairs - 1)]
         order = list(dict.fromkeys(order))
         counts.append(len(order))
@@ -111,7 +122,7 @@
     count = 4 * pairs
     pieces = refs[:count]
     mine, theirs, sums, slots, vecs, weight_hi, weight_lo, turned_hi, turned_lo, cross, shift, *rest = refs[count:]
-    strip_in, strip_out, flipped, spread, bends, sems = rest
+    flipped, spread, bends, sems = rest
     order, counts = groups_of(pairs)
     own_pair = pairs // 2
     part = lax.axis_index("row") % 2
@@ -143,13 +154,16 @@
         for unit in range(PACK)
     ]
 
+    low_lanes = lax.broadcasted_iota(jnp.int32, (BLOCK_ROWS, LANES), 1) < LANES // 2
     for block in range(2 * pairs):
-        for piece in range(PIECES):
-            for comp in range(2):
-                start = EDGE + block * BLOCK_ROWS
-                vecs[0, comp, piece, start : start + BLOCK_ROWS, :] = slots[
-                    block, piece, :BLOCK_ROWS, comp * LANES : (comp + 1) * LANES
-                ]
+        start = EDGE + block * BLOCK_ROWS
+        for comp in range(2):
+            left, middle, right = (
+                slots[block, piece, :BLOCK_ROWS, comp * LANES : (comp + 1) * LANES] for piece in range(PIECES)
+            )
+            placed = (jnp.where(low_lanes, left, right), middle, jnp.where(low_lanes, right, left))
+            for piece in range(PIECES):
+                vecs[0, comp, piece, start : start + BLOCK_ROWS, :] = placed[piece]
 
     def table(row, col, entry):
         start = TABLES + col % HALF_COLS * TABLE_ROWS + entry
@@ -198,51 +212,41 @@
             tiles = [(PACK * group + unit, at) for unit in range(PACK)]
             set_tables(index, 0, tiles, [(row, col + 1) for row, col in tiles])
         else:
-            tiles = [(at, PACK * group + unit) for unit in range(PACK)]
+            tiles = [(at, col) for col in PLACED[group]]
             set_tables(index, 1, tiles, [(row + 1, col) for row, col in tiles])
 
     spread[...] = jnp.zeros_like(spread)
     bends[...] = jnp.zeros_like(bends)
 
-    def seam_batch(indices, first):
+    def seam_group(index, strips, first):
         half = 8 * 2 * PACK
-        gathered = []
-        for index in indices:
-            high, low = split(jnp.concatenate([strip_in[index, comp] for comp in range(2)], axis=0))
-            high = jnp.concatenate([high, high], axis=1)
-            low = jnp.concatenate([low, low], axis=1)
-            left = jnp.concatenate([high * keep[unit] for unit in range(PACK)] + [low * keep[unit] for unit in range(PACK)], axis=0)
-            both = jnp.dot(left, weight_hi[index], preferred_element_type=F32)
-            rest = jnp.dot(left[:half], weight_lo[index], preferred_element_type=F32)
-            gathered.append(both[:half] + both[half:] + rest)
+        high, low = split(jnp.concatenate(strips, axis=0))
+        high = jnp.concatenate([high, high], axis=1)
+        low = jnp.concatenate([low, low], axis=1)
+        left = jnp.concatenate([part * keep[unit] for part in (high, low) for unit in range(PACK)], axis=0)
+        both = jnp.dot(left, weight_hi[index], preferred_element_type=F32)
+        values = both[:half] + both[half:] + jnp.dot(left[:half], weight_lo[index], preferred_element_type=F32)
         pulled = []
-        for index, values in zip(indices, gathered):
-            parts = []
+        for unit in range(PACK):
+            across = cross[index, 8 * unit : 8 * unit + 8, :]
+            for comp in range(2):
+                at = 2 * unit + comp
+                total = jnp.sum(values[8 * at : 8 * at + 8] * across, axis=0, keepdims=True)
+                if first:
+                    total = total - shift[index, at : at + 1, :]
+                pulled.append(total * across)
+        high, low = split(jnp.concatenate(pulled, axis=0))
+        both = jnp.dot(jnp.concatenate([high, low], axis=0), turned_hi[index], preferred_element_type=F32)
+        back = both[:half] + both[half:] + jnp.dot(high, turned_lo[index], preferred_element_type=F32)
+        results = []
+        for comp in range(2):
+            out = None
             for unit in range(PACK):
-                across = cross[index, 8 * unit : 8 * unit + 8, :]
-                for comp in range(2):
-                    at = 2 * unit + comp
-                    total = jnp.sum(values[8 * at : 8 * at + 8] * across, axis=0, keepdims=True)
-                    if first:
-                        total = total - shift[index, at : at + 1, :]
-                    parts.append(total * across)
-            pulled.append(split(jnp.concatenate(parts, axis=0)))
-        numbers = (((1,), (0,)), ((), ()))
-        backs = []
-        for index, (high, low) in zip(indices, pulled):
-            both = lax.dot_general(
-                jnp.concatenate([high, low], axis=0), turned_hi[index], numbers, preferred_element_type=F32
-            )
-            rest = lax.dot_general(high, turned_lo[index], numbers, preferred_element_type=F32)
-            backs.append(both[:half] + both[half:] + rest)
-        for index, back in zip(indices, backs):
-            for comp in range(2):
-                out = None
-                for unit in range(PACK):
-                    at = 8 * (2 * unit + comp)
-                    chosen = jnp.where(near_side, back[at : at + 8, :LANES], back[at : at + 8, LANES:])
-                    out = chosen if out is None else jnp.where(lane8 // GRID == unit, chosen, out)
-                strip_out[index, comp] = out
+                at = 8 * (2 * unit + comp)
+                chosen = jnp.where(near_side, back[at : at + 8, :LANES], back[at : at + 8, LANES:])
+                out = chosen if out is None else jnp.where(lane8 // GRID == unit, chosen, out)
+            results.append(out)
+        return results
 
     sub32 = lax.broadcasted_iota(jnp.int32, (GRID, LANES), 0)
     lane32 = lax.broadcasted_iota(jnp.int32, (GRID, LANES), 1) % GRID
@@ -254,7 +258,7 @@
     def apply(step, scale, own_weight, last_weight):
         for comp in range(2):
             for group in range(pairs):
-                for piece in range(PIECES):
+                for piece in range(PIECES) if step < 2 else (1, 2):
                     start = EDGE + group * LANES
                     flipped[comp, piece * LANES : (piece + 1) * LANES, group * LANES : (group + 1) * LANES] = vecs[
                         step, comp, piece, start : start + LANES, :
@@ -263,64 +267,65 @@
 
         def place(entry):
             direction, at, group = entry
-            return GRID * at + GRID - 8, group, slice(group * LANES, (group + 1) * LANES), direction == 0
+            lanes = slice(group * LANES, (group + 1) * LANES)
+            if direction == 0:
+                return True, position(at) + GRID - 8, position(at + 1), lanes
+            return False, EDGE + GRID * at + GRID - 8, EDGE + GRID * (at + 1), group
+
+        def take_strips(entry):
+            east, before, after, where = place(entry)
+            strips = []
+            for comp in range(2):
+                source = flipped.at[comp, :, where] if east else vecs.at[step, comp, where]
+                strips.append(jnp.where(near_side, source[before : before + 8, :], source[after : after + 8, :]))
+            return strips
 
         for index, entry in enumerate(used):
-            at, piece, lanes, east = place(entry)
+            east, before, after, where = place(entry)
+            if east:
+                results = seam_group(index, take_strips(entry), step == 0)
+                for comp in range(2):
+                    result = scale * results[comp]
+                    spread[comp, before : before + 8, where] = jnp.where(near_side, result, 0.0)
+                    spread[comp, after : after + 8, where] = jnp.where(near_side, 0.0, result)
+        for piece in pieces_at(step):
             for comp in range(2):
-                if east:
-                    before, after = flipped[comp, at : at + 8, lanes], flipped[comp, at + 8 : at + 16, lanes]
-                else:
-                    start = EDGE + at
-                    before = vecs[step, comp, piece, start : start + 8, :]
-                    after = vecs[step, comp, piece, start + 8 : start + 16, :]
-                strip_in[index, comp] = jnp.where(near_side, before, after)
-
-        seam_batch(list(range(len(used))), step == 0)
-
+                for tile in range(4 * pairs):
+                    start = EDGE + tile * GRID
+                    value = vecs[step, comp, piece, start : start + GRID, :]
+                    level = jnp.where(
+                        inner,
+                        vecs[step, comp, piece, start - 1 : start + GRID - 1, :]
+                        + vecs[step, comp, piece, start + 1 : start + GRID + 1, :]
+                        + beside(value),
+                        0.0,
+                    )
+                    bends[comp, piece, tile, EDGE : EDGE + GRID, :] = level
+                    out = (scale * BEND_WEIGHT) * (
+                        bends[comp, piece, tile, EDGE - 1 : EDGE + GRID - 1, :]
+                        + bends[comp, piece, tile, EDGE + 1 : EDGE + GRID + 1, :]
+                        + beside(level)
+                    )
+                    if own_weight:
+                        out = out + own_weight * value
+                    if last_weight:
+                        out = out + last_weight * vecs[step - 1, comp, piece, start : start + GRID, :]
+                    vecs[step + 1, comp, piece, start : start + GRID, :] = out
         for index, entry in enumerate(used):
-            at, piece, lanes, east = place(entry)
-            if east:
+            east, before, after, where = place(entry)
+            if not east:
+                results = seam_group(index, take_strips(entry), step == 0)
                 for comp in range(2):
-                    spread[comp, at : at + 8, lanes] = jnp.where(near_side, strip_out[index, comp], 0.0)
-                    spread[comp, at + 8 : at + 16, lanes] = jnp.where(near_side, 0.0, strip_out[index, comp])
-        for piece in (1,) if step == ITERS else range(PIECES):
+                    result = scale * results[comp]
+                    vecs[step + 1, comp, where, before : before + 8, :] += jnp.where(near_side, result, 0.0)
+                    vecs[step + 1, comp, where, after : after + 8, :] += jnp.where(near_side, 0.0, result)
+        for piece in pieces_at(step):
             for comp in range(2):
                 for group in range(pairs):
-                    turned = spread[
+                    start = EDGE + group * LANES
+                    vecs[step + 1, comp, piece, start : start + LANES, :] += spread[
                         comp, piece * LANES : (piece + 1) * LANES, group * LANES : (group + 1) * LANES
                     ].T
-                    for unit in range(PACK):
-                        tile = PACK * group + unit
-                        start = EDGE + tile * GRID
-                        value = vecs[step, comp, piece, start : start + GRID, :]
-                        level = jnp.where(
-                            inner,
-                            vecs[step, comp, piece, start - 1 : start + GRID - 1, :]
-                            + vecs[step, comp, piece, start + 1 : start + GRID + 1, :]
-                            + beside(value),
-                            0.0,
-                        )
-                        bends[comp, piece, tile, EDGE : EDGE + GRID, :] = level
-                        curved = (
-                            bends[comp, piece, tile, EDGE - 1 : EDGE + GRID - 1, :]
-                            + bends[comp, piece, tile, EDGE + 1 : EDGE + GRID + 1, :]
-                            + beside(level)
-                        )
-                        out = scale * (turned[unit * GRID : (unit + 1) * GRID] + BEND_WEIGHT * curved)
-                        if own_weight:
-                            out = out + own_weight * value
-                        if last_weight:
-                            out = out + last_weight * vecs[step - 1, comp, piece, start : start + GRID, :]
-                        vecs[step + 1, comp, piece, start : start + GRID, :] = out
-        for index, entry in enumerate(used):
-            at, piece, lanes, east = place(entry)
-            if not east:
-                start = EDGE + at
-                for comp in range(2):
-                    result = scale * strip_out[index, comp]
-                    vecs[step + 1, comp, piece, start : start + 8, :] += jnp.where(near_side, result, 0.0)
-                    vecs[step + 1, comp, piece, start + 8 : start + 16, :] += jnp.where(near_side, 0.0, result)
 
     apply(0, -1.0, 0.0, 0.0)
     apply(1, 1.0 / RADIUS, (DAMPING - CENTRE) / RADIUS, 0.0)
@@ -466,8 +471,6 @@
             pltpu.VMEM((groups, SAMPLES, 2 * LANES), BF16),
             pltpu.VMEM((groups, 8 * PACK, SAMPLES), F32),
             pltpu.VMEM((groups, 2 * PACK, SAMPLES), F32),
-            pltpu.VMEM((groups, 2, 8, LANES), F32),
-            pltpu.VMEM((groups, 2, 8, LANES), F32),
             pltpu.VMEM((2, WIDTH, pairs * LANES), F32),
             pltpu.VMEM((2, WIDTH, pairs * LANES), F32),
             pltpu.VMEM((2, PIECES, 4 * pairs, GRID + 2 * EDGE, LANES), F32),

time: 39.9 us -> 38.8 us (0.972)
  Pallas kernels: 11.5 us -> 10.3 us
    pallas_call x1, Pallas kernels: 9.02 us -> 7.9 us  [shards(): pl.pallas_call(lambda *refs: window_kernel(pairs, *refs), out_shape=(part...]
where the time goes in v3:
time: 38.8 us; the launch traced here: 38.6 us
  blocking collectives  11 us (28%)
  Pallas kernels  10.3 us (27%)
  starting transfers between devices  8.41 us (22%)
  waiting for transfers between devices  8.17 us (21%)
  between operations  0.67 us (2%)
    all_to_all x1, blocking collectives, shards(): sums = lax.all_to_all(sums, axes, 0, 0, tiled=True)  11 us
    ppermute x4, starting transfers between devices, shifted(): return lax.ppermute(value, axes, perm)  8.41 us
    ppermute x4, waiting for transfers between devices, shifted(): return lax.ppermute(value, axes, perm)  8.17 us
    pallas_call x1, Pallas kernels, shards(): pl.pallas_call(lambda *refs: window_kernel(pairs, *refs), out_shape=(part...  7.9 us
    pallas_call x1, Pallas kernels, shards(): pl.pallas_call(pack_kernel, out_shape=(jax.ShapeDtypeStruct((2, HALF_ROWS...  1.28 us
    pallas_call x1, Pallas kernels, shards(): pl.pallas_call(final_kernel, out_shape=(out, out), in_specs=[anywhere] *...  1.16 us
  transfers between devices with their start and end apart: 4, of which 2 were waited for; matrix products, arithmetic and copies ran while one was open for 0% of the time, Pallas kernels for 0%

profile of v3, /device:TPU:0, one launch (start us, length us, event | category | flops | bytes accessed | tf_op | source)
XLA Modules:
  0.0 38.6 jit_solution(7111723734767158115)
XLA Ops:
  0.6 1.3 %pack.1 = (f32[2,168,256]{2,1,0:T(8,128)S(1)}, f32[168,256]{1,0:T(8,128)S(1)}, f32[168,256]{1,0:T(8,128)S(1)}) custom-call(f32[2,64,256]{2,1,0:T(8,128)} %refs_3_.3, f32[2,2,2,2048]{3,2,1,0:T(2,128)} %refs_1_.1, s32[4,2,2048]{2,1,0:T(2,128)} %refs_2_.1, s32[4,2,2048]{2,1,0:T(2,128)} %refs_3_.2, s32[4,2,2,2048]{3,2,1,0:T(2,128)} %refs_4_.1, s32[2,2,8]{2,1,0:T(2,128)} %refs_5_.1), custom_call_target="tpu_custom_call" | custom-call | tf_op jit(solution)/shard_map/pack/pallas_call | solution.py:433
  1.9 3.0 %collective-permute-start = (f32[2,168,256]{2,1,0:T(8,128)S(1)}, f32[2,168,256]{2,1,0:T(8,128)S(1)}, u32[]{:S(2)}, u32[]{:S(2)}) collective-permute-start(f32[2,168,256]{2,1,0:T(8,128)S(1)} %get-tuple-element.8.refs_0_), channel_id=1, source_target_pairs={{0,1},{1,0},{2,3},{3,2},{4,5},{5,4},{6,7},{7,6},{8,9},{9,8},{10,11... | collective-permute-start | bytes 1032200 | tf_op jit(solution)/shard_map/ppermute | solution.py:429
  4.9 1.5 %collective-permute-start.1 = (f32[168,256]{1,0:T(8,128)S(1)}, f32[168,256]{1,0:T(8,128)S(1)}, u32[]{:S(2)}, u32[]{:S(2)}) collective-permute-start(f32[168,256]{1,0:T(8,128)S(1)} %get-tuple-element.9), channel_id=1, source_target_pairs={{0,2},{2,4},{3,1},{4,6},{5,3},{6,8},{7,5},{8,10},{9,7},{10,12},{11... | collective-permute-start | bytes 516104 | tf_op jit(solution)/shard_map/ppermute | solution.py:429
  6.4 0.7 %collective-permute-start.2 = (f32[168,256]{1,0:T(8,128)S(1)}, f32[168,256]{1,0:T(8,128)S(1)}, u32[]{:S(2)}, u32[]{:S(2)}) collective-permute-start(f32[168,256]{1,0:T(8,128)S(1)} %get-tuple-element.10), channel_id=1, source_target_pairs={{1,2},{2,1},{3,4},{4,3},{5,6},{6,5},{7,8},{8,7},{9,10},{10,9},{11,... | collective-permute-start | bytes 516104 | tf_op jit(solution)/shard_map/ppermute | solution.py:429
  7.1 0.3 collective-permute-done.1.refs_2_
  7.4 0.0 collective-permute-done.2.refs_3_
  7.4 7.8 %collective-permute-done.refs_1_ = f32[2,168,256]{2,1,0:T(8,128)S(1)} collective-permute-done((f32[2,168,256]{2,1,0:T(8,128)S(1)}, f32[2,168,256]{2,1,0:T(8,128)S(1)}, u32[]{:S(2)}, u32[]{:S(2)}) %collective-permute-start) | collective-permute-done | bytes 344096 | tf_op jit(solution)/shard_map/ppermute | solution.py:429
  15.3 0.0 copy-start
  15.3 7.9 %window.1 = (f32[4,2,64,128]{3,2,1,0:T(8,128)S(1)}, f32[4,2,64,128]{3,2,1,0:T(8,128)S(1)}, f32[32,128]{1,0:T(8,128)S(1)}) custom-call(f32[2,168,256]{2,1,0:T(8,128)S(1)} %get-tuple-element.8.refs_0_, f32[2,168,256]{2,1,0:T(8,128)S(1)} %collective-permute-done.refs_1_, f32[168,256]{1,0:T(8,128)S(1)} %collective-permute-done.1.refs_2_, ...), custom_call_target="tpu_custom_call" | custom-call | tf_op jit(solution)/shard_map/window/pallas_call | solution.py:460
  23.2 3.3 %collective-permute-start.3 = (f32[4,2,64,128]{3,2,1,0:T(8,128)S(1)}, f32[4,2,64,128]{3,2,1,0:T(8,128)S(1)}, u32[]{:S(2)}, u32[]{:S(2)}) collective-permute-start(f32[4,2,64,128]{3,2,1,0:T(8,128)S(1)} %get-tuple-element.13), channel_id=1, source_target_pairs={{0,1},{1,0},{2,3},{3,2},{4,5},{5,4},{6,7},{7,6},{8,9},{9,8},{10,11... | collective-permute-start | bytes 786440 | tf_op jit(solution)/shard_map/ppermute | solution.py:429
  26.4 11.0 %all_to_all.11 = f32[32,1,128]{2,1,0:T(1,128)S(1)} all-to-all(f32[32,1,128]{2,1,0:T(1,128)S(1)} %bitcast.5), channel_id=1, replica_groups=mesh['col'=16,'row'=2] {'col','row'}, dimensions={0} | all-to-all | bytes 32768 | tf_op jit(solution)/shard_map/all_to_all | solution.py:484
  37.4 0.0 collective-permute-done.3.refs_2_
  37.4 0.0 copy-done
  37.4 1.2 %final.1 = (f32[2,64,256]{2,1,0:T(8,128)}, f32[2,64,256]{2,1,0:T(8,128)}) custom-call(f32[32,128]{1,0:T(8,128)S(1)} %bitcast.4, f32[4,2,64,128]{3,2,1,0:T(8,128)S(1)} %get-tuple-element.12.refs_1_, f32[4,2,64,128]{3,2,1,0:T(8,128)S(1)} %collective-permute-done.3.refs_2_, f32[2,64,256]{2,1,0:T(8,128)S(1)} %copy-done), custom_call_target="tpu_custom_call" | custom-call | tf_op jit(solution)/shard_map/final/pallas_call | solution.py:487
Async XLA Ops:
  1.9 13.3 %collective-permute-start = (f32[2,168,256]{2,1,0:T(8,128)S(1)}, f32[2,168,256]{2,1,0:T(8,128)S(1)}, u32[]{:S(2)}, u32[]{:S(2)}) collective-permute-start(f32[2,168,256]{2,1,0:T(8,128)S(1)} %get-tuple-element.8.refs_0_), channel_id=1, source_target_pairs={{0,1},{1,0},{2,3},{3,2},{4,5},{5,4},{6,7},{7,6},{8,9},{9,8},{10,11... | collective-permute-start | bytes 1032200 | tf_op jit(solution)/shard_map/ppermute | solution.py:429
  4.9 2.5 %collective-permute-start.1 = (f32[168,256]{1,0:T(8,128)S(1)}, f32[168,256]{1,0:T(8,128)S(1)}, u32[]{:S(2)}, u32[]{:S(2)}) collective-permute-start(f32[168,256]{1,0:T(8,128)S(1)} %get-tuple-element.9), channel_id=1, source_target_pairs={{0,2},{2,4},{3,1},{4,6},{5,3},{6,8},{7,5},{8,10},{9,7},{10,12},{11... | collective-permute-start | bytes 516104 | tf_op jit(solution)/shard_map/ppermute | solution.py:429
  6.4 1.0 %collective-permute-start.2 = (f32[168,256]{1,0:T(8,128)S(1)}, f32[168,256]{1,0:T(8,128)S(1)}, u32[]{:S(2)}, u32[]{:S(2)}) collective-permute-start(f32[168,256]{1,0:T(8,128)S(1)} %get-tuple-element.10), channel_id=1, source_target_pairs={{1,2},{2,1},{3,4},{4,3},{5,6},{6,5},{7,8},{8,7},{9,10},{10,9},{11,... | collective-permute-start | bytes 516104 | tf_op jit(solution)/shard_map/ppermute | solution.py:429
  15.3 22.2 %copy-start = (f32[2,64,256]{2,1,0:T(8,128)S(1)}, f32[2,64,256]{2,1,0:T(8,128)}, u32[]{:S(2)}) copy-start(f32[2,64,256]{2,1,0:T(8,128)} %refs_3_.3) | copy-start | bytes 393220
  23.2 14.2 %collective-permute-start.3 = (f32[4,2,64,128]{3,2,1,0:T(8,128)S(1)}, f32[4,2,64,128]{3,2,1,0:T(8,128)S(1)}, u32[]{:S(2)}, u32[]{:S(2)}) collective-permute-start(f32[4,2,64,128]{3,2,1,0:T(8,128)S(1)} %get-tuple-element.13), channel_id=1, source_target_pairs={{0,1},{1,0},{2,3},{3,2},{4,5},{5,4},{6,7},{7,6},{8,9},{9,8},{10,11... | collective-permute-start | bytes 786440 | tf_op jit(solution)/shard_map/ppermute | solution.py:429

commit v4 on v3

--- a/solution.py
+++ b/solution.py
@@ -31,7 +31,7 @@
 CENTRE, RADIUS = (HIGH + LOW) / 2, (HIGH - LOW) / 2
 
 BASIS = ITERS + 1
-PAIRS = [(i, j) for i in range(BASIS) for j in range(i, BASIS)]
+PAIRS = [(i, j) for j in range(BASIS) for i in range(min(j, ITERS - 1) + 1)]
 SUM_ROWS = 16
 SUM_LANES = LANES // SUM_ROWS
 EDGE = 8
@@ -330,26 +330,35 @@
     apply(0, -1.0, 0.0, 0.0)
     apply(1, 1.0 / RADIUS, (DAMPING - CENTRE) / RADIUS, 0.0)
     apply(2, 2.0 / RADIUS, 2.0 * (DAMPING - CENTRE) / RADIUS, -1.0)
+    first_row = EDGE + own_pair * 2 * BLOCK_ROWS
+
+    def products(pairs_now):
+        partial = [jnp.zeros((8, LANES), F32) for _ in pairs_now]
+        for comp in range(2):
+            for row in range(first_row, first_row + 2 * BLOCK_ROWS, 8):
+                values = {k: vecs[1 + k, comp, 1, row : row + 8, :] for k in {k for pair in pairs_now for k in pair}}
+                for n, (i, j) in enumerate(pairs_now):
+                    partial[n] = partial[n] + values[i] * values[j]
+        return partial
+
+    def hand_over(k):
+        for comp in range(2):
+            for out, block in ((mine, part), (theirs, 1 - part)):
+                start = pl.multiple_of(first_row + block * BLOCK_ROWS, EDGE)
+                out[k, comp] = vecs[1 + k, comp, 1, pl.ds(start, BLOCK_ROWS), :]
+
+    partial = products([pair for pair in PAIRS if pair[1] < ITERS])
+    for k in range(ITERS):
+        hand_over(k)
     apply(3, 2.0 / RADIUS, 2.0 * (DAMPING - CENTRE) / RADIUS, -1.0)
-
-    first_row = EDGE + own_pair * 2 * BLOCK_ROWS
-    partial = [jnp.zeros((8, LANES), F32) for _ in PAIRS]
-    for comp in range(2):
-        for row in range(first_row, first_row + 2 * BLOCK_ROWS, 8):
-            values = [vecs[1 + k, comp, 1, row : row + 8, :] for k in range(BASIS)]
-            for n, (i, j) in enumerate(PAIRS):
-                partial[n] = partial[n] + values[i] * values[j]
+    partial += products([pair for pair in PAIRS if pair[1] == ITERS])
+    hand_over(ITERS)
     rows = [jnp.sum(value, axis=0, keepdims=True) for value in partial]
     rows.append(jnp.zeros((SUM_ROWS - len(rows), LANES), F32))
     totals = jnp.sum(jnp.concatenate(rows, axis=0), axis=1, keepdims=True)
     slot = lax.broadcasted_iota(jnp.int32, (SUM_ROWS, LANES), 1) // SUM_LANES
     placed = jnp.where(slot == lax.broadcasted_iota(jnp.int32, (SUM_ROWS, LANES), 0), totals, 0.0)
     sums[...] = jnp.broadcast_to(jnp.sum(placed, axis=0, keepdims=True), sums.shape)
-    for k in range(BASIS):
-        for comp in range(2):
-            for out, block in ((mine, part), (theirs, 1 - part)):
-                start = pl.multiple_of(first_row + block * BLOCK_ROWS, EDGE)
-                out[k, comp] = vecs[1 + k, comp, 1, pl.ds(start, BLOCK_ROWS), :]
 
 
 def final_kernel(*refs):

time: 38.8 us -> 38.8 us (level)
  no operation moved by 1% of the time
where the time goes in v4:
time: 38.8 us; the launch traced here: 38.6 us
  blocking collectives  11 us (28%)
  Pallas kernels  10.3 us (27%)
  starting transfers between devices  8.41 us (22%)
  waiting for transfers between devices  8.17 us (21%)
  between operations  0.67 us (2%)
    all_to_all x1, blocking collectives, shards(): sums = lax.all_to_all(sums, axes, 0, 0, tiled=True)  11 us
    ppermute x4, starting transfers between devices, shifted(): return lax.ppermute(value, axes, perm)  8.41 us
    ppermute x4, waiting for transfers between devices, shifted(): return lax.ppermute(value, axes, perm)  8.17 us
    pallas_call x1, Pallas kernels, shards(): pl.pallas_call(lambda *refs: window_kernel(pairs, *refs), out_shape=(part...  7.91 us
    pallas_call x1, Pallas kernels, shards(): pl.pallas_call(pack_kernel, out_shape=(jax.ShapeDtypeStruct((2, HALF_ROWS...  1.28 us
    pallas_call x1, Pallas kernels, shards(): pl.pallas_call(final_kernel, out_shape=(out, out), in_specs=[anywhere] *...  1.16 us
  transfers between devices with their start and end apart: 4, of which 2 were waited for; matrix products, arithmetic and copies ran while one was open for 0% of the time, Pallas kernels for 0%

profile of v4, /device:TPU:0, one launch (start us, length us, event | category | flops | bytes accessed | tf_op | source)
XLA Modules:
  0.0 38.6 jit_solution(13980751689418236220)
XLA Ops:
  0.6 1.3 %pack.1 = (f32[2,168,256]{2,1,0:T(8,128)S(1)}, f32[168,256]{1,0:T(8,128)S(1)}, f32[168,256]{1,0:T(8,128)S(1)}) custom-call(f32[2,64,256]{2,1,0:T(8,128)} %refs_3_.3, f32[2,2,2,2048]{3,2,1,0:T(2,128)} %refs_1_.1, s32[4,2,2048]{2,1,0:T(2,128)} %refs_2_.1, s32[4,2,2048]{2,1,0:T(2,128)} %refs_3_.2, s32[4,2,2,2048]{3,2,1,0:T(2,128)} %refs_4_.1, s32[2,2,8]{2,1,0:T(2,128)} %refs_5_.1), custom_call_target="tpu_custom_call" | custom-call | tf_op jit(solution)/shard_map/pack/pallas_call | solution.py:442
  1.9 3.0 %collective-permute-start = (f32[2,168,256]{2,1,0:T(8,128)S(1)}, f32[2,168,256]{2,1,0:T(8,128)S(1)}, u32[]{:S(2)}, u32[]{:S(2)}) collective-permute-start(f32[2,168,256]{2,1,0:T(8,128)S(1)} %get-tuple-element.8.refs_0_), channel_id=1, source_target_pairs={{0,1},{1,0},{2,3},{3,2},{4,5},{5,4},{6,7},{7,6},{8,9},{9,8},{10,11... | collective-permute-start | bytes 1032200 | tf_op jit(solution)/shard_map/ppermute | solution.py:438
  4.9 1.5 %collective-permute-start.1 = (f32[168,256]{1,0:T(8,128)S(1)}, f32[168,256]{1,0:T(8,128)S(1)}, u32[]{:S(2)}, u32[]{:S(2)}) collective-permute-start(f32[168,256]{1,0:T(8,128)S(1)} %get-tuple-element.9), channel_id=1, source_target_pairs={{0,2},{2,4},{3,1},{4,6},{5,3},{6,8},{7,5},{8,10},{9,7},{10,12},{11... | collective-permute-start | bytes 516104 | tf_op jit(solution)/shard_map/ppermute | solution.py:438
  6.4 0.7 %collective-permute-start.2 = (f32[168,256]{1,0:T(8,128)S(1)}, f32[168,256]{1,0:T(8,128)S(1)}, u32[]{:S(2)}, u32[]{:S(2)}) collective-permute-start(f32[168,256]{1,0:T(8,128)S(1)} %get-tuple-element.10), channel_id=1, source_target_pairs={{1,2},{2,1},{3,4},{4,3},{5,6},{6,5},{7,8},{8,7},{9,10},{10,9},{11,... | collective-permute-start | bytes 516104 | tf_op jit(solution)/shard_map/ppermute | solution.py:438
  7.1 0.3 collective-permute-done.1.refs_2_
  7.4 0.0 collective-permute-done.2.refs_3_
  7.4 7.8 %collective-permute-done.refs_1_ = f32[2,168,256]{2,1,0:T(8,128)S(1)} collective-permute-done((f32[2,168,256]{2,1,0:T(8,128)S(1)}, f32[2,168,256]{2,1,0:T(8,128)S(1)}, u32[]{:S(2)}, u32[]{:S(2)}) %collective-permute-start) | collective-permute-done | bytes 344096 | tf_op jit(solution)/shard_map/ppermute | solution.py:438
  15.3 0.0 copy-start
  15.3 7.9 %window.1 = (f32[4,2,64,128]{3,2,1,0:T(8,128)S(1)}, f32[4,2,64,128]{3,2,1,0:T(8,128)S(1)}, f32[32,128]{1,0:T(8,128)S(1)}) custom-call(f32[2,168,256]{2,1,0:T(8,128)S(1)} %get-tuple-element.8.refs_0_, f32[2,168,256]{2,1,0:T(8,128)S(1)} %collective-permute-done.refs_1_, f32[168,256]{1,0:T(8,128)S(1)} %collective-permute-done.1.refs_2_, ...), custom_call_target="tpu_custom_call" | custom-call | tf_op jit(solution)/shard_map/window/pallas_call | solution.py:469
  23.2 3.3 %collective-permute-start.3 = (f32[4,2,64,128]{3,2,1,0:T(8,128)S(1)}, f32[4,2,64,128]{3,2,1,0:T(8,128)S(1)}, u32[]{:S(2)}, u32[]{:S(2)}) collective-permute-start(f32[4,2,64,128]{3,2,1,0:T(8,128)S(1)} %get-tuple-element.13), channel_id=1, source_target_pairs={{0,1},{1,0},{2,3},{3,2},{4,5},{5,4},{6,7},{7,6},{8,9},{9,8},{10,11... | collective-permute-start | bytes 786440 | tf_op jit(solution)/shard_map/ppermute | solution.py:438
  26.4 11.0 %all_to_all.11 = f32[32,1,128]{2,1,0:T(1,128)S(1)} all-to-all(f32[32,1,128]{2,1,0:T(1,128)S(1)} %bitcast.5), channel_id=1, replica_groups=mesh['col'=16,'row'=2] {'col','row'}, dimensions={0} | all-to-all | bytes 32768 | tf_op jit(solution)/shard_map/all_to_all | solution.py:493
  37.4 0.0 collective-permute-done.3.refs_2_
  37.4 0.0 copy-done
  37.4 1.2 %final.1 = (f32[2,64,256]{2,1,0:T(8,128)}, f32[2,64,256]{2,1,0:T(8,128)}) custom-call(f32[32,128]{1,0:T(8,128)S(1)} %bitcast.4, f32[4,2,64,128]{3,2,1,0:T(8,128)S(1)} %get-tuple-element.12.refs_1_, f32[4,2,64,128]{3,2,1,0:T(8,128)S(1)} %collective-permute-done.3.refs_2_, f32[2,64,256]{2,1,0:T(8,128)S(1)} %copy-done), custom_call_target="tpu_custom_call" | custom-call | tf_op jit(solution)/shard_map/final/pallas_call | solution.py:496
Async XLA Ops:
  1.9 13.3 %collective-permute-start = (f32[2,168,256]{2,1,0:T(8,128)S(1)}, f32[2,168,256]{2,1,0:T(8,128)S(1)}, u32[]{:S(2)}, u32[]{:S(2)}) collective-permute-start(f32[2,168,256]{2,1,0:T(8,128)S(1)} %get-tuple-element.8.refs_0_), channel_id=1, source_target_pairs={{0,1},{1,0},{2,3},{3,2},{4,5},{5,4},{6,7},{7,6},{8,9},{9,8},{10,11... | collective-permute-start | bytes 1032200 | tf_op jit(solution)/shard_map/ppermute | solution.py:438
  4.9 2.5 %collective-permute-start.1 = (f32[168,256]{1,0:T(8,128)S(1)}, f32[168,256]{1,0:T(8,128)S(1)}, u32[]{:S(2)}, u32[]{:S(2)}) collective-permute-start(f32[168,256]{1,0:T(8,128)S(1)} %get-tuple-element.9), channel_id=1, source_target_pairs={{0,2},{2,4},{3,1},{4,6},{5,3},{6,8},{7,5},{8,10},{9,7},{10,12},{11... | collective-permute-start | bytes 516104 | tf_op jit(solution)/shard_map/ppermute | solution.py:438
  6.4 1.0 %collective-permute-start.2 = (f32[168,256]{1,0:T(8,128)S(1)}, f32[168,256]{1,0:T(8,128)S(1)}, u32[]{:S(2)}, u32[]{:S(2)}) collective-permute-start(f32[168,256]{1,0:T(8,128)S(1)} %get-tuple-element.10), channel_id=1, source_target_pairs={{1,2},{2,1},{3,4},{4,3},{5,6},{6,5},{7,8},{8,7},{9,10},{10,9},{11,... | collective-permute-start | bytes 516104 | tf_op jit(solution)/shard_map/ppermute | solution.py:438
  15.3 22.2 %copy-start = (f32[2,64,256]{2,1,0:T(8,128)S(1)}, f32[2,64,256]{2,1,0:T(8,128)}, u32[]{:S(2)}) copy-start(f32[2,64,256]{2,1,0:T(8,128)} %refs_3_.3) | copy-start | bytes 393220
  23.2 14.2 %collective-permute-start.3 = (f32[4,2,64,128]{3,2,1,0:T(8,128)S(1)}, f32[4,2,64,128]{3,2,1,0:T(8,128)S(1)}, u32[]{:S(2)}, u32[]{:S(2)}) collective-permute-start(f32[4,2,64,128]{3,2,1,0:T(8,128)S(1)} %get-tuple-element.13), channel_id=1, source_target_pairs={{0,1},{1,0},{2,3},{3,2},{4,5},{5,4},{6,7},{7,6},{8,9},{9,8},{10,11... | collective-permute-start | bytes 786440 | tf_op jit(solution)/shard_map/ppermute | solution.py:438
